TPU v7x, 256 devices: a whole 4x4x8 slice. The times are simulated.
256 devices in a mesh: grp: 2 (over z_hi), fsdp: 16 (over y, x), dp: 8 (over z_lo, core).
Axes of the slice: x: 4, y: 4, z: 8 (z_hi: 2, z_lo: 4; z = z_hi * 4 + z_lo), core: 2. Of those that a mesh axis runs over, the one named last changes fastest.
Arguments:
- acts: bfloat16 [2, 2432, 2048], P('grp', None, 'dp'), may hold values from -12 to 12
- modulation: float32 [2, 3, 2432], P('grp'), may hold values from -3 to 3
- w_in: bfloat16 [2, 9728, 2432], P('grp', 'fsdp'), may hold values from -0.125 to 0.125
- w_out: bfloat16 [2, 9728, 2432], P('grp', 'fsdp'), may hold values from -0.0625 to 0.0625
- zero_weight: bfloat16 [2432, 2432], P('fsdp'), may hold values from -0.125 to 0.125
- cotangent: bfloat16 [2, 2432, 2048], P('grp', 'fsdp', 'dp'), may hold values from -0.75 to 0.75
Outputs:
- block_out: bfloat16 [2, 2432, 2048], P('grp', 'fsdp', 'dp')
- input_grad: float32 [2, 2432, 2048], P('grp', 'fsdp', 'dp')
- zero_grad: float32 [2432, 2432], P('fsdp')
All inputs are finite; a program needn't handle non-finite values.
Results may differ from a plain program's by a relative error of at most 0.0048.
Values may be sent and summed in bfloat16 or wider, within the bound.
A program may use at most 64 MiB of HBM per device.

v0:
```python
from functools import partial

import jax
import jax.numpy as jnp
from jax import lax
from jax.sharding import PartitionSpec as P

EPSILON = 1e-06


def passed_along(value, axis, by):
    length = lax.axis_size(axis)
    pairs = [(i, i + by) for i in range(length) if 0 <= i + by < length]
    return lax.ppermute(value, axis, pairs)


def layer_norm(values, mod_shift, mod_scale):
    token_mean = jnp.mean(values, axis=0, keepdims=True)
    centred = values - token_mean
    variance = jnp.mean(centred * centred, axis=0, keepdims=True)
    return centred * lax.rsqrt(variance + EPSILON) * (1.0 + mod_scale[:, None]) + mod_shift[:, None]


def contract_rows(weights, columns):
    return lax.dot_general(
        weights, columns, (((0,), (0,)), ((), ())), preferred_element_type=jnp.float32
    )


def sum_features(product):
    return lax.psum(product, "fsdp")


def local(acts, modulation, w_in, w_out, zero_weight, cotangent):
    inputs = acts[0]
    mod_shift = modulation[0, 0]
    mod_scale = modulation[0, 1]
    mod_gate = modulation[0, 2]
    w_first = w_in[0]
    w_second = w_out[0]
    own_grads = cotangent[0]
    feature_count, tokens = inputs.shape
    row_count = own_grads.shape[0]
    half_tokens = tokens // 2
    is_control = lax.axis_index("grp") == 0
    offset = lax.axis_index("fsdp") * row_count
    values = inputs.astype(jnp.float32)
    normed = layer_norm(values, mod_shift, mod_scale).astype(jnp.bfloat16)
    pre_act = jnp.dot(w_first, normed, preferred_element_type=jnp.float32)
    hidden = jax.nn.gelu(pre_act, approximate=True).astype(jnp.bfloat16)
    branch_term = contract_rows(w_second, hidden)
    own_values = lax.dynamic_slice_in_dim(values, offset, row_count, 0)
    own_gate = lax.dynamic_slice_in_dim(mod_gate, offset, row_count, 0)
    empty_rows = jnp.zeros((row_count, tokens), jnp.float32)
    branch = sum_features(branch_term)
    full_mixed = (values + mod_gate[:, None] * branch).astype(jnp.bfloat16)
    arrived = passed_along(full_mixed, "grp", 1)
    control_out = jnp.where(is_control, full_mixed, arrived)
    own_branch = lax.dynamic_slice_in_dim(branch, offset, row_count, 0)
    residual = lax.cond(
        is_control,
        lambda: empty_rows,
        lambda: jnp.dot(zero_weight, control_out, preferred_element_type=jnp.float32),
    )
    block_rows = (own_values + own_gate[:, None] * own_branch + residual).astype(jnp.bfloat16)
    received = passed_along(own_grads, "grp", -1)
    grad_rows = jnp.where(is_control, received, own_grads)
    token_start = jnp.where(is_control, 0, half_tokens).astype(jnp.int32)
    grad_part = lax.dynamic_slice_in_dim(grad_rows, token_start, half_tokens, 1)
    hidden_part = lax.dynamic_slice_in_dim(control_out, token_start, half_tokens, 1)
    zero_term = lax.dot_general(
        grad_part, hidden_part, (((1,), (1,)), ((), ())), preferred_element_type=jnp.float32
    )
    zero_grad = lax.psum(zero_term, ("grp", "dp"))
    carried = lax.cond(
        is_control,
        lambda: contract_rows(zero_weight, received),
        lambda: jnp.zeros((feature_count, tokens), jnp.float32),
    )
    own_rows = lax.dynamic_slice_in_dim(carried, offset, row_count, 0) + own_grads.astype(
        jnp.float32
    )
    upstream = sum_features(lax.dynamic_update_slice_in_dim(carried, own_rows, offset, 0))
    gate_grad = (mod_gate[:, None] * upstream).astype(jnp.bfloat16)
    hidden_grad = jnp.dot(w_second, gate_grad, preferred_element_type=jnp.float32)
    gelu_back = jax.vjp(partial(jax.nn.gelu, approximate=True), pre_act)[1]
    pre_grad = gelu_back(hidden_grad)[0].astype(jnp.bfloat16)
    norm_term = contract_rows(w_first, pre_grad)
    norm_grad = lax.psum(norm_term, "fsdp")
    norm_back = jax.vjp(partial(layer_norm, mod_shift=mod_shift, mod_scale=mod_scale), values)[1]
    input_full = upstream + norm_back(norm_grad)[0]
    input_rows = lax.dynamic_slice_in_dim(input_full, offset, row_count, 0)
    return (block_rows[None], input_rows[None], zero_grad)


def solution(mesh):
    placed = (
        P("grp", None, "dp"),
        P("grp", None, None),
        P("grp", "fsdp", None),
        P("grp", "fsdp", None),
        P("fsdp", None),
        P("grp", "fsdp", "dp"),
    )
    return jax.shard_map(
        local,
        mesh=mesh,
        in_specs=placed,
        out_specs=(P("grp", "fsdp", "dp"), P("grp", "fsdp", "dp"), P("fsdp", None)),
        check_vma=False,
    )
```

profile of v0, /device:TPU:1, one launch (start us, length us, event | category | flops | bytes accessed | tf_op | source)
XLA Modules:
  0.0 453.7 jit_solution(15678255249556649633)
XLA Ops:
  7.2 1.1 copy.20
  8.4 1.3 collective-permute-start.1
  9.7 10.2 %collective-permute-done.1 = bf16[152,256]{0,1:T(8,128)(2,1)S(1)} collective-permute-done((bf16[152,256]{0,1:T(8,128)(2,1)S(1)}, bf16[152,256]{0,1:T(8,128)(2,1)S(1)}, u32[]{:S(2)}, u32[]{:S(2)}) %collective-permute-start.1) | collective-permute-done | bytes 77856 | tf_op jit(solution)/shard_map/ppermute | solution.py:14
  19.8 1.6 conditional.3
  19.8 1.6 fusion.65
  21.5 1.4 copy-done.3
  22.9 0.1 convert_add_fusion
  23.1 1.9 dynamic_update_slice.3
  25.0 2.4 copy.17
  27.4 1.6 convert_reduce_fusion
  29.1 1.8 multiply_reduce_fusion.1
  30.9 3.0 fusion.7
  33.9 0.8 copy-done.5
  34.8 2.7 convolution_bitcast_fusion.1
  37.5 91.8 %all-reduce.5.cloned.1.call-done = f32[2432,256]{0,1:T(8,128)} async-done(((f32[2432,256]{0,1:T(8,128)}), f32[2432,256]{0,1:T(8,128)}) %all-reduce.5.cloned.1.call-update) | async-done | bytes 2490384 | tf_op jit(solution)/shard_map/psum | solution.py:31
  129.2 8.2 %convolution_bitcast_fusion = f32[2432,256]{0,1:T(8,128)} fusion(bf16[1,608,2432]{2,1,0:T(8,128)(2,1)} %param.12, f32[608,256]{1,0:T(8,128)} %copy-done.5, bf16[1,608,2432]{2,1,0:T(8,128)(2,1)S(1)} %copy-done, f32[2432,256]{0,1:T(8,128)} %all-reduce.5.cloned.1.call-done, f32[2432]{0:T(1024)S(1)} %get-tuple-element.37), kind=kOutput, calls=%fused_computation | convolution fusion | flops 1518501888 | bytes 11527680 | tf_op jit(solution)/shard_map/dot_general | solution.py:25
  137.5 121.1 %all-reduce.9.cloned.1.call-done = (f32[2432,256]{0,1:T(8,128)}, f32[2432,256]{0,1:T(8,128)}) async-done(((f32[2432,256]{0,1:T(8,128)}, f32[2432,256]{0,1:T(8,128)}), (f32[2432,256]{0,1:T(8,128)}, f32[2432,256]{0,1:T(8,128)})) %all-reduce.9.cloned.1.call-update) | async-done | bytes 4980752 | tf_op jit(solution)/shard_map/psum | solution.py:31
  258.6 2.8 multiply_reduce_fusion
  261.4 0.4 copy-done.4
  261.8 4.5 fusion.63
  266.3 8.5 %collective-permute-start = (bf16[2432,256]{0,1:T(8,128)(2,1)}, bf16[2432,256]{0,1:T(8,128)(2,1)}, u32[]{:S(2)}, u32[]{:S(2)}) collective-permute-start(bf16[2432,256]{0,1:T(8,128)(2,1)} %get-tuple-element.44), channel_id=1, source_target_pairs={{0,128},{1,129},{2,130},{3,131},{4,132},{5,133},{6,134},{7,135},{8... | collective-permute-start | bytes 3735560 | tf_op jit(solution)/shard_map/ppermute | solution.py:14
  274.8 25.2 %collective-permute-done = bf16[2432,256]{0,1:T(8,128)(2,1)} collective-permute-done((bf16[2432,256]{0,1:T(8,128)(2,1)}, bf16[2432,256]{0,1:T(8,128)(2,1)}, u32[]{:S(2)}, u32[]{:S(2)}) %collective-permute-start) | collective-permute-done | bytes 1245216 | tf_op jit(solution)/shard_map/ppermute | solution.py:14
  300.0 2.5 broadcast_select_fusion
  302.5 2.6 fusion.27
  305.1 0.1 constant_dynamic-slice_fusion
  305.2 3.0 convert_element_type.35
  308.2 1.4 dynamic-slice_add_fusion
  309.6 0.8 copy.24
  310.3 1.3 fusion.48
  311.7 0.7 copy.25
  312.4 132.2 %all-reduce.7.cloned.1.call-done = f32[152,2432]{1,0:T(8,128)} async-done(((f32[152,2432]{1,0:T(8,128)}), f32[152,2432]{1,0:T(8,128)}) %all-reduce.7.cloned.1.call-update) | async-done | bytes 1478672 | tf_op jit(solution)/shard_map/psum | solution.py:74
  444.6 2.6 copy.41
  (24 shorter events, 0.3 us)
Async XLA Ops:
  7.2 27.6 %copy-start = (bf16[1,608,2432]{2,1,0:T(8,128)(2,1)S(1)}, bf16[1,608,2432]{2,1,0:T(8,128)(2,1)}, u32[]{:S(2)}) copy-start(bf16[1,608,2432]{2,1,0:T(8,128)(2,1)} %param.13) | copy-start | bytes 8871940
  7.2 122.1 %all-reduce.5.cloned.1.call-start = ((), (), s32[]{:S(2)}) async-start(), calls=%async_computation | async-start | bytes 4980736 | tf_op jit(solution)/shard_map/psum | solution.py:31
  8.4 11.5 %collective-permute-start.1 = (bf16[152,256]{0,1:T(8,128)(2,1)S(1)}, bf16[152,256]{0,1:T(8,128)(2,1)S(1)}, u32[]{:S(2)}, u32[]{:S(2)}) collective-permute-start(bf16[152,256]{0,1:T(8,128)(2,1)S(1)} %bitcast.63), channel_id=1, source_target_pairs={{128,0},{129,1},{130,2},{131,3},{132,4},{133,5},{134,6},{135,7},{1... | collective-permute-start | bytes 233480 | tf_op jit(solution)/shard_map/ppermute | solution.py:14
  21.5 1.5 copy-start.3
  24.9 5.9 %copy-start.6 = (f32[1,3,2432]{2,0,1:T(1,128)S(1)}, f32[1,3,2432]{2,0,1:T(1,128)}, u32[]{:S(2)}) copy-start(f32[1,3,2432]{2,0,1:T(1,128)} %param.11) | copy-start | bytes 87556
  25.0 233.6 %all-reduce.9.cloned.1.call-start = ((), (), s32[]{:S(2)}) async-start(), calls=%async_computation.2 | async-start | bytes 9961472 | tf_op jit(solution)/shard_map/psum | solution.py:31
  27.4 3.5 copy-start.1
  33.9 0.8 copy-start.5
  137.5 307.1 %all-reduce.7.cloned.1.call-start = ((), (), s32[]{:S(2)}) async-start(), calls=%async_computation.1 | async-start | bytes 2957312 | tf_op jit(solution)/shard_map/psum | solution.py:74
  258.6 2.8 copy-start.2
  258.6 3.2 copy-start.4
  266.3 33.7 %collective-permute-start = (bf16[2432,256]{0,1:T(8,128)(2,1)}, bf16[2432,256]{0,1:T(8,128)(2,1)}, u32[]{:S(2)}, u32[]{:S(2)}) collective-permute-start(bf16[2432,256]{0,1:T(8,128)(2,1)} %get-tuple-element.44), channel_id=1, source_target_pairs={{0,128},{1,129},{2,130},{3,131},{4,132},{5,133},{6,134},{7,135},{8... | collective-permute-start | bytes 3735560 | tf_op jit(solution)/shard_map/ppermute | solution.py:14
Sparse Core Ops, SparseCore 0:
  25.1 104.1 all-reduce.4
  137.6 120.9 all-reduce.8
  305.2 139.3 all-reduce.6
where the time goes:
time: 454 us
  waiting for transfers between devices  380 us (84%)
  other arithmetic  19.1 us (4%)
  matrix products  18.1 us (4%)
  between operations  13.9 us (3%)
  local copies, waits for them, and re-layouts  12.3 us (3%)
  starting transfers between devices  9.88 us (2%)
    psum x2, waiting for transfers between devices, sum_features(): return lax.psum(product, 'fsdp')  213 us
    psum x1, waiting for transfers between devices, local(): zero_grad = lax.psum(zero_term, ('grp', 'dp'))  132 us
    ppermute x2, waiting for transfers between devices, passed_along(): return lax.ppermute(value, axis, pairs)  35.4 us
    dot_general x2, matrix products, contract_rows(): lax.dot_general(weights, columns, (((0,), (0,)), ((), ())), preferred_ele...  10.9 us
    ppermute x2, starting transfers between devices, passed_along(): return lax.ppermute(value, axis, pairs)  9.76 us
    unnamed x18, local copies, waits for them, and re-layouts  9.56 us
  transfers between devices with their start and end apart: 5, of which 5 were waited for; matrix products, arithmetic and copies ran while one was open for 4% of the time, Pallas kernels for 0%

commit v1 on v0

v1 whole, which is shorter than its diff:
```python
from functools import partial

import jax
import jax.numpy as jnp
from jax import lax
from jax.experimental import pallas as pl
from jax.experimental.pallas import tpu as pltpu
from jax.sharding import PartitionSpec as P

MESH = pl.DeviceIdType.MESH
F32 = jnp.float32
BF16 = jnp.bfloat16
EPSILON = 1e-06
D = 2432
B = 152
H = 608
N = 256
L = 128
OWN = 192
GELU_C = 0.7978845608028654
TILES = ((0, 640), (640, 640), (1280, 640), (1920, 512))

C1, C2, B1, B2, G1, G2, O1, O2, N1, N2 = range(10)


def contract_rows(a, b):
    return lax.dot_general(a, b, (((0,), (0,)), ((), ())), preferred_element_type=F32)


def kernel(
    acts_h, mod_h, win_h, wout_h, zw_h, cot_h,
    block_o, grad_o, zero_o,
    acts, mod, win, wout, zw, cot, in_sem,
    cols, xf, normed, pre, dgelu, hidden, T, stat,
    sC, rC1, mC32, mC16, rC2,
    sB, rB1, mB32, mB16, rB2,
    sN, rN1, mN32, mN16, rN2,
    GG, GO, a2d, rows32, up32,
    carr_s, carr_r, co_s, co_r,
    st_s1, st_r1, st_s2, st_r2,
    zf, F16, zr1, H32, H16, zr2, A16, A16b,
    ss, rs, st_ss, st_rs, g_ss, g_rs, c_ss, c_rs, z2_ss, z2_rs, z3_ss, z3_rs,
):
    g = lax.axis_index("grp")
    f = lax.axis_index("fsdp")
    d = lax.axis_index("dp")
    y, x = f // 4, f % 4
    z, c = d // 2, d % 2
    pos = g * 4 + z
    control = g == 0
    base = g == 1

    def at_xy(py, px):
        return (g, py * 4 + px, d)

    def at_z(q):
        return (q // 4, f, (q % 4) * 2 + c)

    sibling = (g, f, z * 2 + (1 - c))
    partner = (1 - g, f, d)

    loads = []
    for i, (src, dst) in enumerate(
        ((cot_h.at[0], cot), (zw_h, zw), (mod_h.at[0], mod), (acts_h.at[0], acts), (win_h.at[0], win), (wout_h.at[0], wout))
    ):
        cp = pltpu.make_async_copy(src, dst, in_sem.at[i])
        cp.start()
        loads.append(cp)
    l_cot, l_zw, l_mod, l_acts, l_win, l_wout = loads

    barrier = pltpu.get_barrier_semaphore()
    for k in (1, 2, 3):
        pl.semaphore_signal(barrier, inc=1, device_id=at_xy(y, (x + k) % 4), device_id_type=MESH)
        pl.semaphore_signal(barrier, inc=1, device_id=at_xy((y + k) % 4, x), device_id_type=MESH)
    for k in range(1, 8):
        pl.semaphore_signal(barrier, inc=1, device_id=at_z((pos + k) % 8), device_id_type=MESH)
    pl.semaphore_signal(barrier, inc=1, device_id=sibling, device_id_type=MESH)

    def remote(src, dst, send, recv, where):
        return pltpu.make_async_remote_copy(
            src_ref=src, dst_ref=dst, send_sem=send, recv_sem=recv, device_id=where, device_id_type=MESH
        )

    HK = [(h, k) for k in (1, 3, 2) for h in (0, 1)]

    def peer_x(k):
        return at_xy(y, (x + k) % 4)

    def peer_y(k):
        return at_xy((y + k) % 4, x)

    def rs1(n, s, r1):
        out = []
        for h, k in HK:
            to = (x + k) % 4 if h == 0 else (y + k) % 4
            where = peer_x(k) if h == 0 else peer_y(k)
            out.append(remote(s.at[h, to], r1.at[h, k - 1], ss.at[n, h, k - 1], rs.at[n, h, k - 1], where))
        return out

    def rs2(n, m16, r2):
        out = []
        for h, k in HK:
            to = (y + k) % 4 if h == 0 else (x + k) % 4
            where = peer_y(k) if h == 0 else peer_x(k)
            out.append(remote(m16.at[h, to], r2.at[h, k - 1], ss.at[n, h, k - 1], rs.at[n, h, k - 1], where))
        return out

    def ag1(n, G):
        out = []
        for h, k in HK:
            blk = G.at[0, x, y] if h == 0 else G.at[1, y, x]
            where = peer_y(k) if h == 0 else peer_x(k)
            out.append(remote(blk, blk, ss.at[n, h, k - 1], rs.at[n, h, k - 1], where))
        return out

    def ag2(n, G):
        out = []
        for h, k in HK:
            blk = G.at[0, x] if h == 0 else G.at[1, y]
            where = peer_x(k) if h == 0 else peer_y(k)
            out.append(remote(blk, blk, ss.at[n, h, k - 1], rs.at[n, h, k - 1], where))
        return out

    def start(copies):
        for cp in copies:
            cp.start()

    def arrived(copies):
        for cp in copies:
            cp.wait_recv()

    def sent(copies):
        for cp in copies:
            cp.wait_send()

    def extract(s):
        def body(i, _):
            blk = T[pl.ds(pl.multiple_of(i * B, 8), B), :]
            s[0, i % 4, i // 4] = blk[:, :L].astype(BF16)
            s[1, i // 4, i % 4] = blk[:, L:].astype(BF16)
            return 0

        lax.fori_loop(0, 16, body, 0)

    def rs_mid(s, r1, m32, m16):
        def body(q, _):
            for h in (0, 1):
                own = x if h == 0 else y
                total = s[h, own, q].astype(F32)
                for k in range(3):
                    total = total + r1[h, k, q].astype(F32)
                m32[h, q] = total
                m16[h, q] = total.astype(BF16)
            return 0

        lax.fori_loop(0, 4, body, 0)

    def rs_last(m32, r2, out):
        for h in (0, 1):
            total = m32[h, y if h == 0 else x]
            for k in range(3):
                total = total + r2[h, k].astype(F32)
            out[:, h * L : (h + 1) * L] = total

    def flatten(G):
        def body(i, _):
            yy, xx = i // 2, 2 * (i % 2)
            rows = pl.ds(pl.multiple_of(i * 2 * B, 16), 2 * B)
            for h in (0, 1):
                p, q = (G[0, xx, yy], G[0, xx + 1, yy]) if h == 0 else (G[1, yy, xx], G[1, yy, xx + 1])
                both = jnp.concatenate([p.astype(F32), q.astype(F32)], axis=0)
                a2d[rows, h * L : (h + 1) * L] = both.astype(BF16)
            return 0

        lax.fori_loop(0, 8, body, 0)

    copies_c1, copies_c2 = rs1(C1, sC, rC1), rs2(C2, mC16, rC2)
    copies_b1, copies_b2 = rs1(B1, sB, rB1), rs2(B2, mB16, rB2)
    copies_n1, copies_n2 = rs1(N1, sN, rN1), rs2(N2, mN16, rN2)
    copies_g1, copies_g2 = ag1(G1, GG), ag2(G2, GG)
    copies_o1, copies_o2 = ag1(O1, GO), ag2(O2, GO)
    carr_copy = remote(carr_s, carr_r, g_ss.at[0], g_rs.at[0], partner)
    co_copy = remote(co_s, co_r, g_ss.at[1], g_rs.at[1], partner)
    st1 = [remote(st_s1, st_r1.at[k - 1], st_ss.at[0, k - 1], st_rs.at[0, k - 1], peer_x(k)) for k in (1, 2, 3)]
    st2 = [remote(st_s2, st_r2.at[k - 1], st_ss.at[1, k - 1], st_rs.at[1, k - 1], peer_y(k)) for k in (1, 2, 3)]
    z1 = remote(F16.at[1 - c], zr1, c_ss.at[0], c_rs.at[0], sibling)
    z2 = [
        remote(H16.at[(pos + k) % 8], zr2.at[z], z2_ss.at[k - 1], z2_rs.at[z], at_z((pos + k) % 8))
        for k in (1, 7, 2, 6, 3, 5, 4)
    ]
    z3 = [
        remote(A16.at[pos], A16.at[pos], z3_ss.at[k - 1], z3_rs.at[k - 1], at_z((pos + k) % 8))
        for k in (1, 7, 2, 6, 3, 5, 4)
    ]
    z4 = remote(A16, A16b, c_ss.at[1], c_rs.at[1], sibling)

    def z2_arrival(zz):
        return remote(H16.at[0], zr2.at[zz], z2_ss.at[0], z2_rs.at[zz], sibling)

    l_cot.wait()
    l_zw.wait()

    @pl.when(base)
    def _():
        for c0, width in TILES:
            T[c0 : c0 + width, :] = contract_rows(zw[:, c0 : c0 + width], cot[...])
        extract(sC)

    pl.semaphore_wait(barrier, 14)

    @pl.when(base)
    def _():
        start(copies_c1)

    l_mod.wait()
    l_acts.wait()

    def column_body(j, _):
        at = pl.ds(pl.multiple_of(j * L, L), L)
        row = lax.broadcasted_iota(jnp.int32, (8, L), 0)
        m = mod[:, at]
        three = jnp.where(row == 0, m[0:1, :], jnp.where(row == 1, 1.0 + m[1:2, :], m[2:3, :]))
        cols[at, 0:8] = jnp.transpose(three)
        return 0

    lax.fori_loop(0, D // L, column_body, 0)

    def fold(v):
        return jnp.sum(v.reshape(L // 8, 8, N), axis=0)

    def sum_body(j, acc):
        at = pl.ds(pl.multiple_of(j * L, L), L)
        v = acts[at, :].astype(F32)
        xf[at, :] = v
        return acc + fold(v)

    zeros8 = jnp.zeros((8, N), F32)
    mean = jnp.sum(lax.fori_loop(0, D // L, sum_body, zeros8), axis=0, keepdims=True) * (1.0 / D)

    def var_body(j, acc):
        at = pl.ds(pl.multiple_of(j * L, L), L)
        v = xf[at, :] - mean
        return acc + fold(v * v)

    variance = jnp.sum(lax.fori_loop(0, D // L, var_body, zeros8), axis=0, keepdims=True) * (1.0 / D)
    rstd = lax.rsqrt(variance + EPSILON)
    stat[0:1, :] = mean
    stat[1:2, :] = rstd

    def norm_body(j, _):
        at = pl.ds(pl.multiple_of(j * L, L), L)
        v = (xf[at, :] - mean) * rstd
        normed[at, :] = (v * cols[at, 1:2] + cols[at, 0:1]).astype(BF16)
        return 0

    lax.fori_loop(0, D // L, norm_body, 0)

    l_win.wait()
    half = H // 2
    for i in range(2):
        pre[i * half : (i + 1) * half, :] = jnp.dot(
            win[i * half : (i + 1) * half, :], normed[...], preferred_element_type=F32
        )

    def gelu_body(j, _):
        at = pl.ds(pl.multiple_of(j * 32, 32), 32)
        v = pre[at, :]
        v2 = v * v
        t = jnp.tanh(GELU_C * (v + 0.044715 * (v2 * v)))
        cdf = 0.5 * (1.0 + t)
        hidden[at, :] = (v * cdf).astype(BF16)
        dgelu[at, :] = cdf + 0.5 * v * (1.0 - t * t) * (GELU_C * (1.0 + 3.0 * 0.044715 * v2))
        return 0

    lax.fori_loop(0, H // 32, gelu_body, 0)
    l_wout.wait()
    for c0, width in TILES:
        T[c0 : c0 + width, :] = contract_rows(wout[:, c0 : c0 + width], hidden[...])
    extract(sB)
    start(copies_b1)

    own_rows = pl.ds(pl.multiple_of(f * B, 8), B)
    gate_rows = cols[own_rows, 2:3]

    def set_gate_grad(up):
        gg = (gate_rows * up).astype(BF16)
        GG[0, x, y] = gg[:, :L]
        GG[1, y, x] = gg[:, L:]

    @pl.when(base)
    def _():
        arrived(copies_c1)
        rs_mid(sC, rC1, mC32, mC16)
        start(copies_c2)
        up = cot[...].astype(F32)
        up32[...] = up
        set_gate_grad(up)
        start(copies_g1)
        arrived(copies_c2)
        rs_last(mC32, rC2, rows32)
        carr_s[...] = rows32[...].astype(BF16)
        carr_copy.start()
        arrived(copies_g1)
        start(copies_g2)

    arrived(copies_b1)
    rs_mid(sB, rB1, mB32, mB16)
    start(copies_b2)
    arrived(copies_b2)
    rs_last(mB32, rB2, rows32)
    rows32[...] = xf[own_rows, :] + gate_rows * rows32[...]

    @pl.when(control)
    def _():
        out = rows32[...].astype(BF16)
        block_o[...] = out
        co_s[...] = out
        co_copy.start()
        carr_copy.wait_recv()
        up = carr_r[...].astype(F32) + cot[...].astype(F32)
        up32[...] = up
        set_gate_grad(up)
        start(copies_g1)
        arrived(copies_g1)
        start(copies_g2)

    arrived(copies_g2)
    flatten(GG)
    for i in range(2):
        hg = jnp.dot(wout[i * half : (i + 1) * half, :], a2d[...], preferred_element_type=F32)
        hidden[i * half : (i + 1) * half, :] = (hg * dgelu[i * half : (i + 1) * half, :]).astype(BF16)
    for c0, width in TILES:
        T[c0 : c0 + width, :] = contract_rows(win[:, c0 : c0 + width], hidden[...])
    extract(sN)

    def stat_body(j, acc):
        at = pl.ds(pl.multiple_of(j * L, L), L)
        v = T[at, :] * cols[at, 1:2]
        xhat = (xf[at, :] - stat[0:1, :]) * stat[1:2, :]
        return acc[0] + fold(v), acc[1] + fold(v * xhat)

    start(copies_n1)
    p1, p2 = lax.fori_loop(0, D // L, stat_body, (zeros8, zeros8))
    st_s1[0:8, :] = p1
    st_s1[8:16, :] = p2
    start(st1)

    @pl.when(base)
    def _():
        co_copy.wait_recv()
        GO[0, x, y] = co_r[:, :L]
        GO[1, y, x] = co_r[:, L:]
        start(copies_o1)
        arrived(copies_o1)
        start(copies_o2)
        arrived(copies_o2)
        flatten(GO)
        zf[19 * B :, :] = jnp.zeros((16 * OWN - 19 * B, L), F32)
        for c0, width in TILES:
            term = lax.dot_general(
                cot[...], a2d[c0 : c0 + width, :], (((1,), (1,)), ((), ())), preferred_element_type=F32
            )
            for t in range(width // L):
                r0 = (c0 // L + t) * B
                zf[r0 : r0 + B, :] = term[:, t * L : (t + 1) * L]

        def flat_body(o, _):
            F16[o // 8, o % 8] = zf[pl.ds(pl.multiple_of(o * OWN, OWN), OWN), :].astype(BF16)
            return 0

        lax.fori_loop(0, 16, flat_body, 0)
        z1.start()
        residual = jnp.dot(zw[...], a2d[...], preferred_element_type=F32)
        block_o[...] = (rows32[...] + residual).astype(BF16)
        z1.wait_recv()

        def pair_body(q, _):
            total = zf[pl.ds(pl.multiple_of((c * 8 + q) * OWN, OWN), OWN), :] + zr1[q].astype(F32)
            H32[q] = total
            H16[q] = total.astype(BF16)
            return 0

        lax.fori_loop(0, 8, pair_body, 0)
        start(z2)

    arrived(copies_n1)
    rs_mid(sN, rN1, mN32, mN16)
    start(copies_n2)
    arrived(st1)
    st_s2[...] = st_s1[...] + st_r1[0] + st_r1[1] + st_r1[2]
    start(st2)
    arrived(copies_n2)
    arrived(st2)
    rs_last(mN32, rN2, rows32)
    both = st_s2[...] + st_r2[0] + st_r2[1] + st_r2[2]
    m1 = jnp.sum(both[0:8, :], axis=0, keepdims=True) * (1.0 / D)
    m2 = jnp.sum(both[8:16, :], axis=0, keepdims=True) * (1.0 / D)
    xhat = (xf[own_rows, :] - stat[0:1, :]) * stat[1:2, :]
    ghat = rows32[...] * cols[own_rows, 1:2]
    grad_o[...] = up32[...] + stat[1:2, :] * (ghat - m1 - xhat * m2)

    @pl.when(base)
    def _():
        for k in (1, 2, 3):
            z2_arrival((z + k) % 4).wait_recv()
        total = H32[pos]
        for k in (1, 2, 3):
            total = total + zr2[(z + k) % 4].astype(F32)
        A16[pos] = total.astype(BF16)

    @pl.when(control)
    def _():
        for k in range(4):
            z2_arrival(k).wait_recv()
        total = zr2[0].astype(F32)
        for k in (1, 2, 3):
            total = total + zr2[k].astype(F32)
        A16[pos] = total.astype(BF16)

    start(z3)
    arrived(z3)
    z4.start()

    def own_body(q, _):
        zf[pl.ds(pl.multiple_of((c * 8 + q) * OWN, OWN), OWN), :] = A16[q].astype(F32)
        return 0

    lax.fori_loop(0, 8, own_body, 0)
    z4.wait_recv()

    def other_body(q, _):
        zf[pl.ds(pl.multiple_of(((1 - c) * 8 + q) * OWN, OWN), OWN), :] = A16b[q].astype(F32)
        return 0

    lax.fori_loop(0, 8, other_body, 0)
    for t in range(19):
        zero_o[:, t * L : (t + 1) * L] = zf[t * B : (t + 1) * B, :].astype(BF16)

    sent(copies_b1 + copies_b2 + copies_g1 + copies_g2 + copies_n1 + copies_n2 + st1 + st2 + z3 + [z4])

    @pl.when(base)
    def _():
        sent(copies_c1 + copies_c2 + copies_o1 + copies_o2 + z2 + [carr_copy, z1])

    @pl.when(control)
    def _():
        co_copy.wait_send()


def local(acts, modulation, w_in, w_out, zero_weight, cotangent):
    vm = pltpu.VMEM
    dma = pltpu.SemaphoreType.DMA

    def rs_bufs():
        return [vm((2, 4, 4, B, L), BF16), vm((2, 3, 4, B, L), BF16), vm((2, 4, B, L), F32), vm((2, 4, B, L), BF16), vm((2, 3, B, L), BF16)]

    scratch = [
        vm((D, N), BF16), vm((3, D), F32), vm((H, D), BF16), vm((H, D), BF16), vm((B, D), BF16), vm((B, N), BF16), dma((6,)),
        vm((D, L), F32), vm((D, N), F32), vm((D, N), BF16), vm((H, N), F32), vm((H, N), F32), vm((H, N), BF16), vm((D, N), F32), vm((8, N), F32),
        *rs_bufs(), *rs_bufs(), *rs_bufs(),
        vm((2, 4, 4, B, L), BF16), vm((2, 4, 4, B, L), BF16), vm((D, N), BF16), vm((B, N), F32), vm((B, N), F32),
        vm((B, N), BF16), vm((B, N), BF16), vm((B, N), BF16), vm((B, N), BF16),
        vm((16, N), F32), vm((3, 16, N), F32), vm((16, N), F32), vm((3, 16, N), F32),
        vm((16 * OWN, L), F32), vm((2, 8, OWN, L), BF16), vm((8, OWN, L), BF16), vm((8, OWN, L), F32), vm((8, OWN, L), BF16),
        vm((4, OWN, L), BF16), vm((8, OWN, L), BF16), vm((8, OWN, L), BF16),
        dma((10, 2, 3)), dma((10, 2, 3)), dma((2, 3)), dma((2, 3)), dma((2,)), dma((2,)), dma((2,)), dma((2,)),
        dma((7,)), dma((4,)), dma((7,)), dma((7,)),
    ]
    block, grad, zero = pl.pallas_call(
        kernel,
        out_shape=(
            jax.ShapeDtypeStruct((B, N), BF16),
            jax.ShapeDtypeStruct((B, N), F32),
            jax.ShapeDtypeStruct((B, D), BF16),
        ),
        in_specs=[pl.BlockSpec(memory_space=pl.ANY)] * 6,
        out_specs=[pl.BlockSpec(memory_space=pltpu.VMEM)] * 3,
        scratch_shapes=scratch,
        compiler_params=pltpu.CompilerParams(
            collective_id=0, has_side_effects=True, vmem_limit_bytes=60 * 2**20
        ),
    )(acts, modulation, w_in, w_out, zero_weight, cotangent)
    return block[None], grad[None], zero.astype(F32)


def solution(mesh):
    placed = (
        P("grp", None, "dp"),
        P("grp", None, None),
        P("grp", "fsdp", None),
        P("grp", "fsdp", None),
        P("fsdp", None),
        P("grp", "fsdp", "dp"),
    )
    return jax.shard_map(
        local,
        mesh=mesh,
        in_specs=placed,
        out_specs=(P("grp", "fsdp", "dp"), P("grp", "fsdp", "dp"), P("fsdp", None)),
        check_vma=False,
    )
```

time: 454 us -> 98.4 us (0.22)
  waiting for transfers between devices: 380 us -> 0 us
  Pallas kernels: 0 us -> 90.7 us
  matrix products: 18.1 us -> 0 us
  other arithmetic: 19.1 us -> 2.33 us
  between operations: 13.9 us -> 0.64 us
  starting transfers between devices: 9.88 us -> 0 us
  local copies, waits for them, and re-layouts: 12.3 us -> 4.49 us
    psum x3 -> x0, waiting for transfers between devices: 345 us -> none  [the longest x2 213 us: sum_features(): return lax.psum(product, 'fsdp')]
    pallas_call x0 -> x1, Pallas kernels: none -> 90.7 us  [local(): pl.pallas_call(kernel, out_shape=(jax.ShapeDtypeStruct((B, N), BF16), jax...]
    ppermute x2 -> x0, waiting for transfers between devices: 35.4 us -> none  [passed_along(): return lax.ppermute(value, axis, pairs)]
    dot_general x4 -> x0, matrix products: 16.5 us -> none  [the longest x2 10.9 us: contract_rows(): lax.dot_general(weights, columns, (((0,), (0,)), ((), ())), preferred_ele...]
    reduce_sum x4 -> x0, other arithmetic: 10.7 us -> none  [the longest x1 4.52 us: layer_norm(): centred = values - token_mean]
    ppermute x2 -> x0, starting transfers between devices: 9.76 us -> none  [passed_along(): return lax.ppermute(value, axis, pairs)]
    unnamed x18 -> x3, local copies, waits for them, and re-layouts: 9.56 us -> 4.49 us
  transfers between devices with their start and end apart: 5 -> 0, of which waited for: 5 -> 0; matrix products, arithmetic and copies ran while one was open for 4% -> 0% of each run, Pallas kernels for 0% -> 0%
where the time goes in v1:
time: 98.4 us; the launch traced here: 98.1 us
  Pallas kernels  90.7 us (92%)
  local copies, waits for them, and re-layouts  4.49 us (5%)
  other arithmetic  2.33 us (2%)
    pallas_call x1, Pallas kernels, local(): pl.pallas_call(kernel, out_shape=(jax.ShapeDtypeStruct((B, N), BF16), jax...  90.7 us
    unnamed x3, local copies, waits for them, and re-layouts  4.49 us
    convert_element_type x1, other arithmetic, local(): return (block[None], grad[None], zero.astype(F32))  2.33 us

profile of v1, /device:TPU:1, one launch (start us, length us, event | category | flops | bytes accessed | tf_op | source)
XLA Modules:
  0.0 98.1 jit_solution(18213948250243523766)
XLA Ops:
  0.6 1.4 %copy.9.mod_h = f32[1,3,2432]{2,1,0:T(4,128)} copy(f32[1,3,2432]{2,0,1:T(1,128)} %param.7) | data formatting | bytes 58368 | tf_op args[1]
  2.0 90.7 %shard_map.85 = (bf16[152,256]{1,0:T(8,128)(2,1)}, f32[152,256]{1,0:T(8,128)}, bf16[152,2432]{1,0:T(8,128)(2,1)}) custom-call(bf16[1,2432,256]{2,1,0:T(8,128)(2,1)} %acts_h.1, f32[1,3,2432]{2,1,0:T(4,128)} %copy.9.mod_h, bf16[1,608,2432]{2,1,0:T(8,128)(2,1)} %win_h.1, bf16[1,608,2432]{2,1,0:T(8,128)(2,1)} %wout_h.1, bf16[152,2432]{1,0:T(8,128)(2,1)} %zw_h.1, ...), custom_call_target="tpu_custom_call" | custom-call | tf_op jit(solution)/shard_map/pallas_call | solution.py:469
  92.7 2.3 %convert_element_type.3 = f32[152,2432]{1,0:T(8,128)} convert(bf16[152,2432]{1,0:T(8,128)(2,1)} %get-tuple-element.8) | non-fusion elementwise | flops 369664 | bytes 2217984 | tf_op jit(solution)/shard_map/convert_element_type | solution.py:483
  95.0 1.5 %copy.12 = bf16[1,152,256]{2,1,0:T(8,128)(2,1)} copy(bf16[1,152,256]{2,1,0:T(8,128)(2,1)} %bitcast.3) | data formatting | bytes 155648
  96.5 1.6 %copy.13 = f32[1,152,256]{2,1,0:T(8,128)} copy(f32[1,152,256]{2,1,0:T(8,128)} %bitcast.2) | data formatting | bytes 311296

commit v2 on v1

--- a/solution.py
+++ b/solution.py
@@ -29,7 +29,7 @@
 
 def kernel(
     acts_h, mod_h, win_h, wout_h, zw_h, cot_h,
-    block_o, grad_o, zero_o,
+    block_o, grad_o, A16,
     acts, mod, win, wout, zw, cot, in_sem,
     cols, xf, normed, pre, dgelu, hidden, T, stat,
     sC, rC1, mC32, mC16, rC2,
@@ -38,7 +38,7 @@
     GG, GO, a2d, rows32, up32,
     carr_s, carr_r, co_s, co_r,
     st_s1, st_r1, st_s2, st_r2,
-    zf, F16, zr1, H32, H16, zr2, A16, A16b,
+    cot1_r, zf, F16, zr1, H32, H16, zr2,
     ss, rs, st_ss, st_rs, g_ss, g_rs, c_ss, c_rs, z2_ss, z2_rs, z3_ss, z3_rs,
 ):
     g = lax.axis_index("grp")
@@ -61,7 +61,7 @@
 
     loads = []
     for i, (src, dst) in enumerate(
-        ((cot_h.at[0], cot), (zw_h, zw), (mod_h.at[0], mod), (acts_h.at[0], acts), (win_h.at[0], win), (wout_h.at[0], wout))
+        ((cot_h.at[0], cot), (zw_h, zw), (mod_h, mod), (acts_h.at[0], acts), (win_h.at[0], win), (wout_h.at[0], wout))
     ):
         cp = pltpu.make_async_copy(src, dst, in_sem.at[i])
         cp.start()
@@ -181,6 +181,7 @@
     copies_o1, copies_o2 = ag1(O1, GO), ag2(O2, GO)
     carr_copy = remote(carr_s, carr_r, g_ss.at[0], g_rs.at[0], partner)
     co_copy = remote(co_s, co_r, g_ss.at[1], g_rs.at[1], partner)
+    cot_copy = remote(cot, cot1_r, g_ss.at[2], g_rs.at[2], partner)
     st1 = [remote(st_s1, st_r1.at[k - 1], st_ss.at[0, k - 1], st_rs.at[0, k - 1], peer_x(k)) for k in (1, 2, 3)]
     st2 = [remote(st_s2, st_r2.at[k - 1], st_ss.at[1, k - 1], st_rs.at[1, k - 1], peer_y(k)) for k in (1, 2, 3)]
     z1 = remote(F16.at[1 - c], zr1, c_ss.at[0], c_rs.at[0], sibling)
@@ -189,10 +190,10 @@
         for k in (1, 7, 2, 6, 3, 5, 4)
     ]
     z3 = [
-        remote(A16.at[pos], A16.at[pos], z3_ss.at[k - 1], z3_rs.at[k - 1], at_z((pos + k) % 8))
+        remote(A16.at[c, pos], A16.at[c, pos], z3_ss.at[k - 1], z3_rs.at[k - 1], at_z((pos + k) % 8))
         for k in (1, 7, 2, 6, 3, 5, 4)
     ]
-    z4 = remote(A16, A16b, c_ss.at[1], c_rs.at[1], sibling)
+    z4 = remote(A16.at[c], A16.at[c], c_ss.at[1], c_rs.at[1], sibling)
 
     def z2_arrival(zz):
         return remote(H16.at[0], zr2.at[zz], z2_ss.at[0], z2_rs.at[zz], sibling)
@@ -211,6 +212,7 @@
     @pl.when(base)
     def _():
         start(copies_c1)
+        cot_copy.start()
 
     l_mod.wait()
     l_acts.wait()
@@ -218,8 +220,7 @@
     def column_body(j, _):
         at = pl.ds(pl.multiple_of(j * L, L), L)
         row = lax.broadcasted_iota(jnp.int32, (8, L), 0)
-        m = mod[:, at]
-        three = jnp.where(row == 0, m[0:1, :], jnp.where(row == 1, 1.0 + m[1:2, :], m[2:3, :]))
+        three = jnp.where(row == 0, mod[0, :, at], jnp.where(row == 1, 1.0 + mod[1, :, at], mod[2, :, at]))
         cols[at, 0:8] = jnp.transpose(three)
         return 0
 
@@ -277,7 +278,10 @@
     for c0, width in TILES:
         T[c0 : c0 + width, :] = contract_rows(wout[:, c0 : c0 + width], hidden[...])
     extract(sB)
-    start(copies_b1)
+
+    @pl.when(control)
+    def _():
+        start(copies_b1)
 
     own_rows = pl.ds(pl.multiple_of(f * B, 8), B)
     gate_rows = cols[own_rows, 2:3]
@@ -300,6 +304,7 @@
         rs_last(mC32, rC2, rows32)
         carr_s[...] = rows32[...].astype(BF16)
         carr_copy.start()
+        start(copies_b1)
         arrived(copies_g1)
         start(copies_g2)
 
@@ -316,22 +321,74 @@
         block_o[...] = out
         co_s[...] = out
         co_copy.start()
+        GO[0, x, y] = out[:, :L]
+        GO[1, y, x] = out[:, L:]
+        start(copies_o1)
         carr_copy.wait_recv()
         up = carr_r[...].astype(F32) + cot[...].astype(F32)
         up32[...] = up
         set_gate_grad(up)
         start(copies_g1)
+        arrived(copies_o1)
+        start(copies_o2)
         arrived(copies_g1)
         start(copies_g2)
+        cot_copy.wait_recv()
+        zf[19 * B :, :] = jnp.zeros((16 * OWN - 19 * B, L), F32)
+
+        arrived(copies_o2)
+        flatten(GO)
+        for c0, width in TILES:
+            term = lax.dot_general(
+                cot1_r[...], a2d[c0 : c0 + width, :], (((1,), (1,)), ((), ())), preferred_element_type=F32
+            )
+            for t in range(width // L):
+                r0 = (c0 // L + t) * B
+                zf[r0 : r0 + B, :] = term[:, t * L : (t + 1) * L]
+
+        def flat_body(o, _):
+            F16[o // 8, o % 8] = zf[pl.ds(pl.multiple_of(o * OWN, OWN), OWN), :].astype(BF16)
+            return 0
+
+        lax.fori_loop(0, 16, flat_body, 0)
+        z1.start()
+
+    @pl.when(base)
+    def _():
+        co_copy.wait_recv()
+        GO[0, x, y] = co_r[:, :L]
+        GO[1, y, x] = co_r[:, L:]
+        start(copies_o1)
 
     arrived(copies_g2)
     flatten(GG)
+
+    @pl.when(control)
+    def _():
+        z1.wait_recv()
+
+        def pair_body(q, _):
+            total = zf[pl.ds(pl.multiple_of((c * 8 + q) * OWN, OWN), OWN), :] + zr1[q].astype(F32)
+            H32[q] = total
+            H16[q] = total.astype(BF16)
+            return 0
+
+        lax.fori_loop(0, 8, pair_body, 0)
+        start(z2)
+
     for i in range(2):
         hg = jnp.dot(wout[i * half : (i + 1) * half, :], a2d[...], preferred_element_type=F32)
         hidden[i * half : (i + 1) * half, :] = (hg * dgelu[i * half : (i + 1) * half, :]).astype(BF16)
+
+    @pl.when(base)
+    def _():
+        arrived(copies_o1)
+        start(copies_o2)
+
     for c0, width in TILES:
         T[c0 : c0 + width, :] = contract_rows(win[:, c0 : c0 + width], hidden[...])
     extract(sN)
+    start(copies_n1)
 
     def stat_body(j, acc):
         at = pl.ds(pl.multiple_of(j * L, L), L)
@@ -339,49 +396,30 @@
         xhat = (xf[at, :] - stat[0:1, :]) * stat[1:2, :]
         return acc[0] + fold(v), acc[1] + fold(v * xhat)
 
-    start(copies_n1)
     p1, p2 = lax.fori_loop(0, D // L, stat_body, (zeros8, zeros8))
     st_s1[0:8, :] = p1
     st_s1[8:16, :] = p2
     start(st1)
 
-    @pl.when(base)
-    def _():
-        co_copy.wait_recv()
-        GO[0, x, y] = co_r[:, :L]
-        GO[1, y, x] = co_r[:, L:]
-        start(copies_o1)
-        arrived(copies_o1)
-        start(copies_o2)
-        arrived(copies_o2)
-        flatten(GO)
-        zf[19 * B :, :] = jnp.zeros((16 * OWN - 19 * B, L), F32)
-        for c0, width in TILES:
-            term = lax.dot_general(
-                cot[...], a2d[c0 : c0 + width, :], (((1,), (1,)), ((), ())), preferred_element_type=F32
-            )
-            for t in range(width // L):
-                r0 = (c0 // L + t) * B
-                zf[r0 : r0 + B, :] = term[:, t * L : (t + 1) * L]
-
-        def flat_body(o, _):
-            F16[o // 8, o % 8] = zf[pl.ds(pl.multiple_of(o * OWN, OWN), OWN), :].astype(BF16)
-            return 0
-
-        lax.fori_loop(0, 16, flat_body, 0)
-        z1.start()
-        residual = jnp.dot(zw[...], a2d[...], preferred_element_type=F32)
-        block_o[...] = (rows32[...] + residual).astype(BF16)
-        z1.wait_recv()
-
-        def pair_body(q, _):
-            total = zf[pl.ds(pl.multiple_of((c * 8 + q) * OWN, OWN), OWN), :] + zr1[q].astype(F32)
-            H32[q] = total
-            H16[q] = total.astype(BF16)
-            return 0
-
-        lax.fori_loop(0, 8, pair_body, 0)
-        start(z2)
+    @pl.when(control)
+    def _():
+        for k in (1, 2, 3):
+            z2_arrival((z + k) % 4).wait_recv()
+        total = H32[pos]
+        for k in (1, 2, 3):
+            total = total + zr2[(z + k) % 4].astype(F32)
+        A16[c, pos] = total.astype(BF16)
+
+    @pl.when(base)
+    def _():
+        for k in range(4):
+            z2_arrival(k).wait_recv()
+        total = zr2[0].astype(F32)
+        for k in (1, 2, 3):
+            total = total + zr2[k].astype(F32)
+        A16[c, pos] = total.astype(BF16)
+
+    start(z3)
 
     arrived(copies_n1)
     rs_mid(sN, rN1, mN32, mN16)
@@ -389,6 +427,14 @@
     arrived(st1)
     st_s2[...] = st_s1[...] + st_r1[0] + st_r1[1] + st_r1[2]
     start(st2)
+
+    @pl.when(base)
+    def _():
+        arrived(copies_o2)
+        flatten(GO)
+        residual = jnp.dot(zw[...], a2d[...], preferred_element_type=F32)
+        block_o[...] = (rows32[...] + residual).astype(BF16)
+
     arrived(copies_n2)
     arrived(st2)
     rs_last(mN32, rN2, rows32)
@@ -399,52 +445,33 @@
     ghat = rows32[...] * cols[own_rows, 1:2]
     grad_o[...] = up32[...] + stat[1:2, :] * (ghat - m1 - xhat * m2)
 
-    @pl.when(base)
-    def _():
-        for k in (1, 2, 3):
-            z2_arrival((z + k) % 4).wait_recv()
-        total = H32[pos]
-        for k in (1, 2, 3):
-            total = total + zr2[(z + k) % 4].astype(F32)
-        A16[pos] = total.astype(BF16)
-
-    @pl.when(control)
-    def _():
-        for k in range(4):
-            z2_arrival(k).wait_recv()
-        total = zr2[0].astype(F32)
-        for k in (1, 2, 3):
-            total = total + zr2[k].astype(F32)
-        A16[pos] = total.astype(BF16)
-
-    start(z3)
     arrived(z3)
     z4.start()
-
-    def own_body(q, _):
-        zf[pl.ds(pl.multiple_of((c * 8 + q) * OWN, OWN), OWN), :] = A16[q].astype(F32)
+    z4.wait_recv()
+
+    sent(copies_b1 + copies_b2 + copies_g1 + copies_g2 + copies_o1 + copies_o2 + copies_n1 + copies_n2)
+    sent(st1 + st2 + z3 + [z4])
+
+    @pl.when(base)
+    def _():
+        sent(copies_c1 + copies_c2 + [carr_copy, cot_copy])
+
+    @pl.when(control)
+    def _():
+        sent(z2 + [co_copy, z1])
+
+
+def finish(block, grad, flat, block_o, grad_o, zero_o, zf):
+    block_o[0] = block[...]
+    grad_o[0] = grad[...]
+
+    def body(o, _):
+        zf[pl.ds(pl.multiple_of(o * OWN, OWN), OWN), :] = flat[o // 8, o % 8].astype(F32)
         return 0
 
-    lax.fori_loop(0, 8, own_body, 0)
-    z4.wait_recv()
-
-    def other_body(q, _):
-        zf[pl.ds(pl.multiple_of(((1 - c) * 8 + q) * OWN, OWN), OWN), :] = A16b[q].astype(F32)
-        return 0
-
-    lax.fori_loop(0, 8, other_body, 0)
+    lax.fori_loop(0, 16, body, 0)
     for t in range(19):
-        zero_o[:, t * L : (t + 1) * L] = zf[t * B : (t + 1) * B, :].astype(BF16)
-
-    sent(copies_b1 + copies_b2 + copies_g1 + copies_g2 + copies_n1 + copies_n2 + st1 + st2 + z3 + [z4])
-
-    @pl.when(base)
-    def _():
-        sent(copies_c1 + copies_c2 + copies_o1 + copies_o2 + z2 + [carr_copy, z1])
-
-    @pl.when(control)
-    def _():
-        co_copy.wait_send()
+        zero_o[:, t * L : (t + 1) * L] = zf[t * B : (t + 1) * B, :]
 
 
 def local(acts, modulation, w_in, w_out, zero_weight, cotangent):
@@ -455,23 +482,23 @@
         return [vm((2, 4, 4, B, L), BF16), vm((2, 3, 4, B, L), BF16), vm((2, 4, B, L), F32), vm((2, 4, B, L), BF16), vm((2, 3, B, L), BF16)]
 
     scratch = [
-        vm((D, N), BF16), vm((3, D), F32), vm((H, D), BF16), vm((H, D), BF16), vm((B, D), BF16), vm((B, N), BF16), dma((6,)),
+        vm((D, N), BF16), vm((3, 1, D), F32), vm((H, D), BF16), vm((H, D), BF16), vm((B, D), BF16), vm((B, N), BF16), dma((6,)),
         vm((D, L), F32), vm((D, N), F32), vm((D, N), BF16), vm((H, N), F32), vm((H, N), F32), vm((H, N), BF16), vm((D, N), F32), vm((8, N), F32),
         *rs_bufs(), *rs_bufs(), *rs_bufs(),
         vm((2, 4, 4, B, L), BF16), vm((2, 4, 4, B, L), BF16), vm((D, N), BF16), vm((B, N), F32), vm((B, N), F32),
         vm((B, N), BF16), vm((B, N), BF16), vm((B, N), BF16), vm((B, N), BF16),
         vm((16, N), F32), vm((3, 16, N), F32), vm((16, N), F32), vm((3, 16, N), F32),
-        vm((16 * OWN, L), F32), vm((2, 8, OWN, L), BF16), vm((8, OWN, L), BF16), vm((8, OWN, L), F32), vm((8, OWN, L), BF16),
-        vm((4, OWN, L), BF16), vm((8, OWN, L), BF16), vm((8, OWN, L), BF16),
-        dma((10, 2, 3)), dma((10, 2, 3)), dma((2, 3)), dma((2, 3)), dma((2,)), dma((2,)), dma((2,)), dma((2,)),
+        vm((B, N), BF16), vm((16 * OWN, L), F32), vm((2, 8, OWN, L), BF16), vm((8, OWN, L), BF16), vm((8, OWN, L), F32), vm((8, OWN, L), BF16),
+        vm((4, OWN, L), BF16),
+        dma((10, 2, 3)), dma((10, 2, 3)), dma((2, 3)), dma((2, 3)), dma((3,)), dma((3,)), dma((2,)), dma((2,)),
         dma((7,)), dma((4,)), dma((7,)), dma((7,)),
     ]
-    block, grad, zero = pl.pallas_call(
+    parts = pl.pallas_call(
         kernel,
         out_shape=(
             jax.ShapeDtypeStruct((B, N), BF16),
             jax.ShapeDtypeStruct((B, N), F32),
-            jax.ShapeDtypeStruct((B, D), BF16),
+            jax.ShapeDtypeStruct((2, 8, OWN, L), BF16),
         ),
         in_specs=[pl.BlockSpec(memory_space=pl.ANY)] * 6,
         out_specs=[pl.BlockSpec(memory_space=pltpu.VMEM)] * 3,
@@ -479,8 +506,19 @@
         compiler_params=pltpu.CompilerParams(
             collective_id=0, has_side_effects=True, vmem_limit_bytes=60 * 2**20
         ),
-    )(acts, modulation, w_in, w_out, zero_weight, cotangent)
-    return block[None], grad[None], zero.astype(F32)
+    )(acts, jnp.transpose(modulation, (1, 0, 2)), w_in, w_out, zero_weight, cotangent)
+    return pl.pallas_call(
+        finish,
+        out_shape=(
+            jax.ShapeDtypeStruct((1, B, N), BF16),
+            jax.ShapeDtypeStruct((1, B, N), F32),
+            jax.ShapeDtypeStruct((B, D), F32),
+        ),
+        in_specs=[pl.BlockSpec(memory_space=pltpu.VMEM)] * 3,
+        out_specs=[pl.BlockSpec(memory_space=pltpu.VMEM)] * 3,
+        scratch_shapes=[vm((16 * OWN, L), F32)],
+        compiler_params=pltpu.CompilerParams(vmem_limit_bytes=16 * 2**20),
+    )(*parts)
 
 
 def solution(mesh):

time: 98.4 us -> 83 us (0.84)
  Pallas kernels: 90.7 us -> 79.3 us
  other arithmetic: 2.33 us -> 0 us
  local copies, waits for them, and re-layouts: 4.49 us -> 2.92 us
    pallas_call x1, Pallas kernels: 90.7 us -> 77.8 us  [local(): pl.pallas_call(kernel, out_shape=(jax.ShapeDtypeStruct((B, N), BF16), jax...]
    convert_element_type x1 -> x0, other arithmetic: 2.33 us -> none  [local(): return (block[None], grad[None], zero.astype(F32))]
    unnamed x3 -> x6, local copies, waits for them, and re-layouts: 4.49 us -> 2.92 us
    pallas_call x0 -> x1, Pallas kernels: none -> 1.5 us  [local(): pl.pallas_call(finish, out_shape=(jax.ShapeDtypeStruct((1, B, N), BF16),...]
where the time goes in v2:
time: 83 us; the launch traced here: 82.9 us
  Pallas kernels  79.3 us (96%)
  local copies, waits for them, and re-layouts  2.92 us (4%)
    pallas_call x1, Pallas kernels, local(): pl.pallas_call(kernel, out_shape=(jax.ShapeDtypeStruct((B, N), BF16), jax...  77.8 us
    unnamed x6, local copies, waits for them, and re-layouts  2.92 us

profile of v2, /device:TPU:1, one launch (start us, length us, event | category | flops | bytes accessed | tf_op | source)
XLA Modules:
  0.0 82.9 jit_solution(11567528121594238234)
XLA Ops:
  0.6 77.8 %shard_map.85 = (bf16[152,256]{1,0:T(8,128)(2,1)}, f32[152,256]{1,0:T(8,128)}, bf16[2,8,192,128]{3,2,1,0:T(8,128)(2,1)}) custom-call(bf16[1,2432,256]{2,1,0:T(8,128)(2,1)} %acts_h.1, f32[3,1,2432]{2,1,0:T(1,128)} %bitcast.1, bf16[1,608,2432]{2,1,0:T(8,128)(2,1)} %win_h.1, bf16[1,608,2432]{2,1,0:T(8,128)(2,1)} %wout_h.1, bf16[152,2432]{1,0:T(8,128)(2,1)} %zw_h.1, ...), custom_call_target="tpu_custom_call" | custom-call | tf_op jit(solution)/shard_map/pallas_call | solution.py:496
  78.4 0.0 copy-start
  78.4 1.1 %copy-done = bf16[2,8,192,128]{3,2,1,0:T(8,128)(2,1)S(1)} copy-done((bf16[2,8,192,128]{3,2,1,0:T(8,128)(2,1)S(1)}, bf16[2,8,192,128]{3,2,1,0:T(8,128)(2,1)}, u32[]{:S(2)}) %copy-start) | copy-done | bytes 786456
  79.6 0.0 copy-start.1
  79.6 0.9 %copy-done.1 = f32[152,256]{1,0:T(8,128)S(1)} copy-done((f32[152,256]{1,0:T(8,128)S(1)}, f32[152,256]{1,0:T(8,128)}, u32[]{:S(2)}) %copy-start.1) | copy-done | bytes 155672
  80.5 0.0 copy-start.2
  80.5 0.9 %copy-done.2 = bf16[152,256]{1,0:T(8,128)(2,1)S(1)} copy-done((bf16[152,256]{1,0:T(8,128)(2,1)S(1)}, bf16[152,256]{1,0:T(8,128)(2,1)}, u32[]{:S(2)}) %copy-start.2) | copy-done | bytes 77848
  81.4 1.5 %shard_map.86 = (bf16[1,152,256]{2,1,0:T(8,128)(2,1)}, f32[1,152,256]{2,1,0:T(8,128)}, f32[152,2432]{1,0:T(8,128)}) custom-call(bf16[152,256]{1,0:T(8,128)(2,1)S(1)} %copy-done.2, f32[152,256]{1,0:T(8,128)S(1)} %copy-done.1, bf16[2,8,192,128]{3,2,1,0:T(8,128)(2,1)S(1)} %copy-done), custom_call_target="tpu_custom_call" | custom-call | tf_op jit(solution)/shard_map/pallas_call | solution.py:510
Async XLA Ops:
  78.4 1.1 %copy-start = (bf16[2,8,192,128]{3,2,1,0:T(8,128)(2,1)S(1)}, bf16[2,8,192,128]{3,2,1,0:T(8,128)(2,1)}, u32[]{:S(2)}) copy-start(bf16[2,8,192,128]{3,2,1,0:T(8,128)(2,1)} %get-tuple-element.8.flat) | copy-start | bytes 2359300
  79.6 0.9 %copy-start.1 = (f32[152,256]{1,0:T(8,128)S(1)}, f32[152,256]{1,0:T(8,128)}, u32[]{:S(2)}) copy-start(f32[152,256]{1,0:T(8,128)} %get-tuple-element.7.grad) | copy-start | bytes 466948
  80.5 0.9 %copy-start.2 = (bf16[152,256]{1,0:T(8,128)(2,1)S(1)}, bf16[152,256]{1,0:T(8,128)(2,1)}, u32[]{:S(2)}) copy-start(bf16[152,256]{1,0:T(8,128)(2,1)} %get-tuple-element.6.block) | copy-start | bytes 233476

commit v3 on v2

--- a/solution.py
+++ b/solution.py
@@ -31,7 +31,7 @@
     acts_h, mod_h, win_h, wout_h, zw_h, cot_h,
     block_o, grad_o, A16,
     acts, mod, win, wout, zw, cot, in_sem,
-    cols, xf, normed, pre, dgelu, hidden, T, stat,
+    parts, cols, xf, normed, pre, dgelu, hidden, T, stat,
     sC, rC1, mC32, mC16, rC2,
     sB, rB1, mB32, mB16, rB2,
     sN, rN1, mN32, mN16, rN2,
@@ -59,14 +59,22 @@
     sibling = (g, f, z * 2 + (1 - c))
     partner = (1 - g, f, d)
 
-    loads = []
-    for i, (src, dst) in enumerate(
-        ((cot_h.at[0], cot), (zw_h, zw), (mod_h, mod), (acts_h.at[0], acts), (win_h.at[0], win), (wout_h.at[0], wout))
-    ):
-        cp = pltpu.make_async_copy(src, dst, in_sem.at[i])
-        cp.start()
-        loads.append(cp)
-    l_cot, l_zw, l_mod, l_acts, l_win, l_wout = loads
+    loads = [
+        pltpu.make_async_copy(src, dst, in_sem.at[i])
+        for i, (src, dst) in enumerate(
+            ((mod_h, mod), (cot_h.at[0], cot), (zw_h, zw), (acts_h.at[0], acts), (win_h.at[0], win), (wout_h.at[0], wout))
+        )
+    ]
+    l_mod, l_cot, l_zw, l_acts, l_win, l_wout = loads
+    l_mod.start()
+    l_cot.start()
+
+    @pl.when(base)
+    def _():
+        l_zw.start()
+
+    l_acts.start()
+    l_win.start()
 
     barrier = pltpu.get_barrier_semaphore()
     for k in (1, 2, 3):
@@ -189,24 +197,49 @@
         remote(H16.at[(pos + k) % 8], zr2.at[z], z2_ss.at[k - 1], z2_rs.at[z], at_z((pos + k) % 8))
         for k in (1, 7, 2, 6, 3, 5, 4)
     ]
-    z3 = [
-        remote(A16.at[c, pos], A16.at[c, pos], z3_ss.at[k - 1], z3_rs.at[k - 1], at_z((pos + k) % 8))
-        for k in (1, 7, 2, 6, 3, 5, 4)
+    def z3_copy(i, blk, q):
+        return remote(blk, blk, z3_ss.at[i], z3_rs.at[i], at_z(q % 8))
+
+    below, above = (pos + 6) % 8, (pos + 2) % 8
+    hw = OWN // 2
+    near = [z3_copy(i, A16.at[c, pos], pos + by) for i, by in enumerate((1, 7, 2, 6))]
+    far = [
+        z3_copy(4, A16.at[c, below], pos + 1),
+        z3_copy(5, A16.at[c, above], pos + 7),
+        z3_copy(6, A16.at[c, below, pl.ds(0, hw)], pos + 2),
+        z3_copy(7, A16.at[c, above, pl.ds(hw, hw)], pos + 6),
     ]
-    z4 = remote(A16.at[c], A16.at[c], c_ss.at[1], c_rs.at[1], sibling)
+    z4 = [remote(A16.at[c, (pos + k) % 8], A16.at[c, (pos + k) % 8], c_ss.at[1 + k], c_rs.at[1 + k], sibling) for k in range(8)]
 
     def z2_arrival(zz):
         return remote(H16.at[0], zr2.at[zz], z2_ss.at[0], z2_rs.at[zz], sibling)
 
     l_cot.wait()
-    l_zw.wait()
-
-    @pl.when(base)
-    def _():
+
+    @pl.when(base)
+    def _():
+        l_zw.wait()
         for c0, width in TILES:
             T[c0 : c0 + width, :] = contract_rows(zw[:, c0 : c0 + width], cot[...])
         extract(sC)
 
+    l_mod.wait()
+    row = lax.broadcasted_iota(jnp.int32, (16, L), 0)
+    for j in range(D // L):
+        at = slice(j * L, (j + 1) * L)
+        value = jnp.zeros((16, L), F32)
+        for n, m in enumerate((1.0 + mod[1, :, at], mod[0, :, at], mod[2, :, at])):
+            high = m.astype(BF16).astype(F32)
+            middle = (m - high).astype(BF16).astype(F32)
+            for k, part in enumerate((high, middle, (m - high) - middle)):
+                value = jnp.where(row == 3 * n + k, part, value)
+        parts[:, at] = value.astype(BF16)
+    which = lax.broadcasted_iota(jnp.int32, (16, 3 * L), 0) // 3
+    column = lax.broadcasted_iota(jnp.int32, (16, 3 * L), 1) // L
+    select = jnp.where(which == column, 1.0, 0.0).astype(BF16)
+    for c0, width in TILES:
+        cols[c0 : c0 + width, :] = contract_rows(parts[:, c0 : c0 + width], select)
+
     pl.semaphore_wait(barrier, 14)
 
     @pl.when(base)
@@ -214,47 +247,32 @@
         start(copies_c1)
         cot_copy.start()
 
-    l_mod.wait()
-    l_acts.wait()
-
-    def column_body(j, _):
-        at = pl.ds(pl.multiple_of(j * L, L), L)
-        row = lax.broadcasted_iota(jnp.int32, (8, L), 0)
-        three = jnp.where(row == 0, mod[0, :, at], jnp.where(row == 1, 1.0 + mod[1, :, at], mod[2, :, at]))
-        cols[at, 0:8] = jnp.transpose(three)
-        return 0
-
-    lax.fori_loop(0, D // L, column_body, 0)
+    def twice(v):
+        return jnp.concatenate([v, v], axis=1)
 
     def fold(v):
         return jnp.sum(v.reshape(L // 8, 8, N), axis=0)
 
-    def sum_body(j, acc):
-        at = pl.ds(pl.multiple_of(j * L, L), L)
-        v = acts[at, :].astype(F32)
-        xf[at, :] = v
-        return acc + fold(v)
-
-    zeros8 = jnp.zeros((8, N), F32)
-    mean = jnp.sum(lax.fori_loop(0, D // L, sum_body, zeros8), axis=0, keepdims=True) * (1.0 / D)
-
-    def var_body(j, acc):
-        at = pl.ds(pl.multiple_of(j * L, L), L)
-        v = xf[at, :] - mean
-        return acc + fold(v * v)
-
-    variance = jnp.sum(lax.fori_loop(0, D // L, var_body, zeros8), axis=0, keepdims=True) * (1.0 / D)
+    l_acts.wait()
+    l_wout.start()
+    total = jnp.zeros((8, N), F32)
+    for j in range(D // L):
+        v = acts[j * L : (j + 1) * L, :].astype(F32)
+        xf[j * L : (j + 1) * L, :] = v
+        total = total + fold(v)
+    mean = jnp.sum(total, axis=0, keepdims=True) * (1.0 / D)
+    total = jnp.zeros((8, N), F32)
+    for j in range(D // L):
+        v = xf[j * L : (j + 1) * L, :] - mean
+        total = total + fold(v * v)
+    variance = jnp.sum(total, axis=0, keepdims=True) * (1.0 / D)
     rstd = lax.rsqrt(variance + EPSILON)
     stat[0:1, :] = mean
     stat[1:2, :] = rstd
-
-    def norm_body(j, _):
-        at = pl.ds(pl.multiple_of(j * L, L), L)
+    for j in range(D // L):
+        at = slice(j * L, (j + 1) * L)
         v = (xf[at, :] - mean) * rstd
-        normed[at, :] = (v * cols[at, 1:2] + cols[at, 0:1]).astype(BF16)
-        return 0
-
-    lax.fori_loop(0, D // L, norm_body, 0)
+        normed[at, :] = (v * twice(cols[at, :L]) + twice(cols[at, L : 2 * L])).astype(BF16)
 
     l_win.wait()
     half = H // 2
@@ -275,16 +293,34 @@
 
     lax.fori_loop(0, H // 32, gelu_body, 0)
     l_wout.wait()
-    for c0, width in TILES:
-        T[c0 : c0 + width, :] = contract_rows(wout[:, c0 : c0 + width], hidden[...])
-    extract(sB)
-
-    @pl.when(control)
-    def _():
-        start(copies_b1)
+
+    def produce(n, weights, s, r1, send):
+        for yy, (c0, width) in enumerate(TILES):
+            T[c0 : c0 + width, :] = contract_rows(weights[:, c0 : c0 + width], hidden[...])
+            for xx in range(4):
+                blk = T[(yy * 4 + xx) * B : (yy * 4 + xx + 1) * B, :]
+                s[0, xx, yy] = blk[:, :L].astype(BF16)
+                s[1, yy, xx] = blk[:, L:].astype(BF16)
+
+            @pl.when(send)
+            def _():
+                for k in (1, 3, 2):
+                    to = (x + k) % 4
+                    remote(
+                        s.at[0, to, yy], r1.at[0, k - 1, yy], ss.at[n, 0, k - 1], rs.at[n, 0, k - 1], peer_x(k)
+                    ).start()
+
+            @pl.when(jnp.logical_and(send, y != yy))
+            def _():
+                k = (yy + 4 - y) % 4
+                remote(
+                    s.at[1, yy], r1.at[1, k - 1], ss.at[n, 1, k - 1], rs.at[n, 1, k - 1], at_xy(yy, x)
+                ).start()
+
+    produce(B1, wout, sB, rB1, control)
 
     own_rows = pl.ds(pl.multiple_of(f * B, 8), B)
-    gate_rows = cols[own_rows, 2:3]
+    gate_rows = twice(cols[own_rows, 2 * L :])
 
     def set_gate_grad(up):
         gg = (gate_rows * up).astype(BF16)
@@ -331,12 +367,12 @@
         start(copies_g1)
         arrived(copies_o1)
         start(copies_o2)
+        cot_copy.wait_recv()
+        zf[19 * B :, :] = jnp.zeros((16 * OWN - 19 * B, L), F32)
+
+        arrived(copies_o2)
         arrived(copies_g1)
         start(copies_g2)
-        cot_copy.wait_recv()
-        zf[19 * B :, :] = jnp.zeros((16 * OWN - 19 * B, L), F32)
-
-        arrived(copies_o2)
         flatten(GO)
         for c0, width in TILES:
             term = lax.dot_general(
@@ -360,9 +396,6 @@
         GO[1, y, x] = co_r[:, L:]
         start(copies_o1)
 
-    arrived(copies_g2)
-    flatten(GG)
-
     @pl.when(control)
     def _():
         z1.wait_recv()
@@ -376,6 +409,8 @@
         lax.fori_loop(0, 8, pair_body, 0)
         start(z2)
 
+    arrived(copies_g2)
+    flatten(GG)
     for i in range(2):
         hg = jnp.dot(wout[i * half : (i + 1) * half, :], a2d[...], preferred_element_type=F32)
         hidden[i * half : (i + 1) * half, :] = (hg * dgelu[i * half : (i + 1) * half, :]).astype(BF16)
@@ -385,18 +420,14 @@
         arrived(copies_o1)
         start(copies_o2)
 
-    for c0, width in TILES:
-        T[c0 : c0 + width, :] = contract_rows(win[:, c0 : c0 + width], hidden[...])
-    extract(sN)
-    start(copies_n1)
-
-    def stat_body(j, acc):
-        at = pl.ds(pl.multiple_of(j * L, L), L)
-        v = T[at, :] * cols[at, 1:2]
-        xhat = (xf[at, :] - stat[0:1, :]) * stat[1:2, :]
-        return acc[0] + fold(v), acc[1] + fold(v * xhat)
-
-    p1, p2 = lax.fori_loop(0, D // L, stat_body, (zeros8, zeros8))
+    produce(N1, win, sN, rN1, g >= 0)
+    p1 = jnp.zeros((8, N), F32)
+    p2 = jnp.zeros((8, N), F32)
+    for j in range(D // L):
+        at = slice(j * L, (j + 1) * L)
+        v = T[at, :] * twice(cols[at, :L])
+        p1 = p1 + fold(v)
+        p2 = p2 + fold(v * ((xf[at, :] - stat[0:1, :]) * stat[1:2, :]))
     st_s1[0:8, :] = p1
     st_s1[8:16, :] = p2
     start(st1)
@@ -419,7 +450,8 @@
             total = total + zr2[k].astype(F32)
         A16[c, pos] = total.astype(BF16)
 
-    start(z3)
+    start(near)
+    z4[0].start()
 
     arrived(copies_n1)
     rs_mid(sN, rN1, mN32, mN16)
@@ -435,6 +467,9 @@
         residual = jnp.dot(zw[...], a2d[...], preferred_element_type=F32)
         block_o[...] = (rows32[...] + residual).astype(BF16)
 
+    arrived(near)
+    start(far)
+    start(z4[1:3] + z4[6:8])
     arrived(copies_n2)
     arrived(st2)
     rs_last(mN32, rN2, rows32)
@@ -442,15 +477,15 @@
     m1 = jnp.sum(both[0:8, :], axis=0, keepdims=True) * (1.0 / D)
     m2 = jnp.sum(both[8:16, :], axis=0, keepdims=True) * (1.0 / D)
     xhat = (xf[own_rows, :] - stat[0:1, :]) * stat[1:2, :]
-    ghat = rows32[...] * cols[own_rows, 1:2]
+    ghat = rows32[...] * twice(cols[own_rows, :L])
     grad_o[...] = up32[...] + stat[1:2, :] * (ghat - m1 - xhat * m2)
 
-    arrived(z3)
-    z4.start()
-    z4.wait_recv()
+    arrived(far)
+    start(z4[3:6])
+    arrived(z4)
 
     sent(copies_b1 + copies_b2 + copies_g1 + copies_g2 + copies_o1 + copies_o2 + copies_n1 + copies_n2)
-    sent(st1 + st2 + z3 + [z4])
+    sent(st1 + st2 + near + far + z4)
 
     @pl.when(base)
     def _():
@@ -461,17 +496,28 @@
         sent(z2 + [co_copy, z1])
 
 
-def finish(block, grad, flat, block_o, grad_o, zero_o, zf):
-    block_o[0] = block[...]
-    grad_o[0] = grad[...]
+def finish(block, grad, flat, block_o, grad_o, zero_o, flat_v, zf, rows, sem):
+    copies = [
+        pltpu.make_async_copy(flat, flat_v, sem.at[0]),
+        pltpu.make_async_copy(block, block_o.at[0], sem.at[1]),
+        pltpu.make_async_copy(grad, grad_o.at[0], sem.at[2]),
+    ]
+    for cp in copies:
+        cp.start()
+    copies[0].wait()
 
     def body(o, _):
-        zf[pl.ds(pl.multiple_of(o * OWN, OWN), OWN), :] = flat[o // 8, o % 8].astype(F32)
+        zf[pl.ds(pl.multiple_of(o * OWN, OWN), OWN), :] = flat_v[o // 8, o % 8].astype(F32)
         return 0
 
     lax.fori_loop(0, 16, body, 0)
     for t in range(19):
-        zero_o[:, t * L : (t + 1) * L] = zf[t * B : (t + 1) * B, :]
+        rows[:, t * L : (t + 1) * L] = zf[t * B : (t + 1) * B, :]
+    out = pltpu.make_async_copy(rows, zero_o, sem.at[3])
+    out.start()
+    out.wait()
+    copies[1].wait()
+    copies[2].wait()
 
 
 def local(acts, modulation, w_in, w_out, zero_weight, cotangent):
@@ -483,17 +529,17 @@
 
     scratch = [
         vm((D, N), BF16), vm((3, 1, D), F32), vm((H, D), BF16), vm((H, D), BF16), vm((B, D), BF16), vm((B, N), BF16), dma((6,)),
-        vm((D, L), F32), vm((D, N), F32), vm((D, N), BF16), vm((H, N), F32), vm((H, N), F32), vm((H, N), BF16), vm((D, N), F32), vm((8, N), F32),
+        vm((16, D), BF16), vm((D, 3 * L), F32), vm((D, N), F32), vm((D, N), BF16), vm((H, N), F32), vm((H, N), F32), vm((H, N), BF16), vm((D, N), F32), vm((8, N), F32),
         *rs_bufs(), *rs_bufs(), *rs_bufs(),
         vm((2, 4, 4, B, L), BF16), vm((2, 4, 4, B, L), BF16), vm((D, N), BF16), vm((B, N), F32), vm((B, N), F32),
         vm((B, N), BF16), vm((B, N), BF16), vm((B, N), BF16), vm((B, N), BF16),
         vm((16, N), F32), vm((3, 16, N), F32), vm((16, N), F32), vm((3, 16, N), F32),
         vm((B, N), BF16), vm((16 * OWN, L), F32), vm((2, 8, OWN, L), BF16), vm((8, OWN, L), BF16), vm((8, OWN, L), F32), vm((8, OWN, L), BF16),
         vm((4, OWN, L), BF16),
-        dma((10, 2, 3)), dma((10, 2, 3)), dma((2, 3)), dma((2, 3)), dma((3,)), dma((3,)), dma((2,)), dma((2,)),
-        dma((7,)), dma((4,)), dma((7,)), dma((7,)),
+        dma((10, 2, 3)), dma((10, 2, 3)), dma((2, 3)), dma((2, 3)), dma((3,)), dma((3,)), dma((9,)), dma((9,)),
+        dma((7,)), dma((4,)), dma((8,)), dma((8,)),
     ]
-    parts = pl.pallas_call(
+    results = pl.pallas_call(
         kernel,
         out_shape=(
             jax.ShapeDtypeStruct((B, N), BF16),
@@ -514,11 +560,11 @@
             jax.ShapeDtypeStruct((1, B, N), F32),
             jax.ShapeDtypeStruct((B, D), F32),
         ),
-        in_specs=[pl.BlockSpec(memory_space=pltpu.VMEM)] * 3,
-        out_specs=[pl.BlockSpec(memory_space=pltpu.VMEM)] * 3,
-        scratch_shapes=[vm((16 * OWN, L), F32)],
-        compiler_params=pltpu.CompilerParams(vmem_limit_bytes=16 * 2**20),
-    )(*parts)
+        in_specs=[pl.BlockSpec(memory_space=pl.ANY)] * 3,
+        out_specs=[pl.BlockSpec(memory_space=pl.ANY)] * 3,
+        scratch_shapes=[vm((2, 8, OWN, L), BF16), vm((16 * OWN, L), F32), vm((B, D), F32), dma((4,))],
+        compiler_params=pltpu.CompilerParams(vmem_limit_bytes=60 * 2**20),
+    )(*results)
 
 
 def solution(mesh):

time: 83 us -> 78 us (0.940)
  local copies, waits for them, and re-layouts: 2.92 us -> 0 us
  Pallas kernels: 79.3 us -> 77.2 us
    pallas_call x1, Pallas kernels: 77.8 us -> 69 us  [local(): pl.pallas_call(kernel, out_shape=(jax.ShapeDtypeStruct((B, N), BF16), jax...]
    pallas_call x1, Pallas kernels: 1.5 us -> 8.21 us  [local(): pl.pallas_call(finish, out_shape=(jax.ShapeDtypeStruct((1, B, N), BF16),...]
    unnamed x6 -> x0, local copies, waits for them, and re-layouts: 2.92 us -> none
where the time goes in v3:
time: 78 us; the launch traced here: 77.9 us
  Pallas kernels  77.2 us (99%)
    pallas_call x1, Pallas kernels, local(): pl.pallas_call(kernel, out_shape=(jax.ShapeDtypeStruct((B, N), BF16), jax...  69 us
    pallas_call x1, Pallas kernels, local(): pl.pallas_call(finish, out_shape=(jax.ShapeDtypeStruct((1, B, N), BF16),...  8.21 us

profile of v3, /device:TPU:1, one launch (start us, length us, event | category | flops | bytes accessed | tf_op | source)
XLA Modules:
  0.0 77.9 jit_solution(2979992955332710344)
XLA Ops:
  0.6 69.0 %shard_map.85 = (bf16[152,256]{1,0:T(8,128)(2,1)}, f32[152,256]{1,0:T(8,128)}, bf16[2,8,192,128]{3,2,1,0:T(8,128)(2,1)}) custom-call(bf16[1,2432,256]{2,1,0:T(8,128)(2,1)} %acts_h.1, f32[3,1,2432]{2,1,0:T(1,128)} %bitcast.1, bf16[1,608,2432]{2,1,0:T(8,128)(2,1)} %win_h.1, bf16[1,608,2432]{2,1,0:T(8,128)(2,1)} %wout_h.1, bf16[152,2432]{1,0:T(8,128)(2,1)} %zw_h.1, ...), custom_call_target="tpu_custom_call" | custom-call | tf_op jit(solution)/shard_map/pallas_call | solution.py:542
  69.6 8.2 %shard_map.86 = (bf16[1,152,256]{2,1,0:T(8,128)(2,1)}, f32[1,152,256]{2,1,0:T(8,128)}, f32[152,2432]{1,0:T(8,128)}) custom-call(bf16[152,256]{1,0:T(8,128)(2,1)} %get-tuple-element.6.block, f32[152,256]{1,0:T(8,128)} %get-tuple-element.7.grad, bf16[2,8,192,128]{3,2,1,0:T(8,128)(2,1)} %get-tuple-element.8.flat), custom_call_target="tpu_custom_call" | custom-call | tf_op jit(solution)/shard_map/pallas_call | solution.py:556

commit v4 on v3

--- a/solution.py
+++ b/solution.py
@@ -16,7 +16,7 @@
 H = 608
 N = 256
 L = 128
-OWN = 192
+OWN = 96
 GELU_C = 0.7978845608028654
 TILES = ((0, 640), (640, 640), (1280, 640), (1920, 512))
 
@@ -39,7 +39,7 @@
     carr_s, carr_r, co_s, co_r,
     st_s1, st_r1, st_s2, st_r2,
     cot1_r, zf, F16, zr1, H32, H16, zr2,
-    ss, rs, st_ss, st_rs, g_ss, g_rs, c_ss, c_rs, z2_ss, z2_rs, z3_ss, z3_rs,
+    ss, rs, st_ss, st_rs, g_ss, g_rs, c_ss, c_rs, z2_ss, z2_rs, z3_ss, z3_rs, z4_ss, z4_rs,
 ):
     g = lax.axis_index("grp")
     f = lax.axis_index("fsdp")
@@ -192,27 +192,44 @@
     cot_copy = remote(cot, cot1_r, g_ss.at[2], g_rs.at[2], partner)
     st1 = [remote(st_s1, st_r1.at[k - 1], st_ss.at[0, k - 1], st_rs.at[0, k - 1], peer_x(k)) for k in (1, 2, 3)]
     st2 = [remote(st_s2, st_r2.at[k - 1], st_ss.at[1, k - 1], st_rs.at[1, k - 1], peer_y(k)) for k in (1, 2, 3)]
-    z1 = remote(F16.at[1 - c], zr1, c_ss.at[0], c_rs.at[0], sibling)
+    z1 = [remote(F16.at[e, 1 - c], zr1.at[e], c_ss.at[e], c_rs.at[e], sibling) for e in (0, 1)]
     z2 = [
-        remote(H16.at[(pos + k) % 8], zr2.at[z], z2_ss.at[k - 1], z2_rs.at[z], at_z((pos + k) % 8))
-        for k in (1, 7, 2, 6, 3, 5, 4)
+        [
+            remote(
+                H16.at[e, (pos + k) % 8], zr2.at[e, z], z2_ss.at[e, k - 1], z2_rs.at[e, z], at_z((pos + k) % 8)
+            )
+            for k in (1, 7, 2, 6, 3, 5, 4)
+        ]
+        for e in (0, 1)
     ]
-    def z3_copy(i, blk, q):
-        return remote(blk, blk, z3_ss.at[i], z3_rs.at[i], at_z(q % 8))
+
+    def z3_copy(e, i, blk, q):
+        return remote(blk, blk, z3_ss.at[e, i], z3_rs.at[e, i], at_z(q % 8))
 
     below, above = (pos + 6) % 8, (pos + 2) % 8
     hw = OWN // 2
-    near = [z3_copy(i, A16.at[c, pos], pos + by) for i, by in enumerate((1, 7, 2, 6))]
+    near = [[z3_copy(e, i, A16.at[e, c, pos], pos + by) for i, by in enumerate((1, 7, 2, 6))] for e in (0, 1)]
     far = [
-        z3_copy(4, A16.at[c, below], pos + 1),
-        z3_copy(5, A16.at[c, above], pos + 7),
-        z3_copy(6, A16.at[c, below, pl.ds(0, hw)], pos + 2),
-        z3_copy(7, A16.at[c, above, pl.ds(hw, hw)], pos + 6),
+        [
+            z3_copy(e, 4, A16.at[e, c, below], pos + 1),
+            z3_copy(e, 5, A16.at[e, c, above], pos + 7),
+            z3_copy(e, 6, A16.at[e, c, below, pl.ds(0, hw)], pos + 2),
+            z3_copy(e, 7, A16.at[e, c, above, pl.ds(hw, hw)], pos + 6),
+        ]
+        for e in (0, 1)
     ]
-    z4 = [remote(A16.at[c, (pos + k) % 8], A16.at[c, (pos + k) % 8], c_ss.at[1 + k], c_rs.at[1 + k], sibling) for k in range(8)]
-
-    def z2_arrival(zz):
-        return remote(H16.at[0], zr2.at[zz], z2_ss.at[0], z2_rs.at[zz], sibling)
+    z4 = [
+        [
+            remote(
+                A16.at[e, c, (pos + k) % 8], A16.at[e, c, (pos + k) % 8], z4_ss.at[e, k], z4_rs.at[e, k], sibling
+            )
+            for k in range(8)
+        ]
+        for e in (0, 1)
+    ]
+
+    def z2_arrival(e, zz):
+        return remote(H16.at[e, 0], zr2.at[e, zz], z2_ss.at[e, 0], z2_rs.at[e, zz], sibling)
 
     l_cot.wait()
 
@@ -222,6 +239,13 @@
         for c0, width in TILES:
             T[c0 : c0 + width, :] = contract_rows(zw[:, c0 : c0 + width], cot[...])
         extract(sC)
+
+    pl.semaphore_wait(barrier, 14)
+
+    @pl.when(base)
+    def _():
+        start(copies_c1)
+        cot_copy.start()
 
     l_mod.wait()
     row = lax.broadcasted_iota(jnp.int32, (16, L), 0)
@@ -239,13 +263,6 @@
     select = jnp.where(which == column, 1.0, 0.0).astype(BF16)
     for c0, width in TILES:
         cols[c0 : c0 + width, :] = contract_rows(parts[:, c0 : c0 + width], select)
-
-    pl.semaphore_wait(barrier, 14)
-
-    @pl.when(base)
-    def _():
-        start(copies_c1)
-        cot_copy.start()
 
     def twice(v):
         return jnp.concatenate([v, v], axis=1)
@@ -368,7 +385,7 @@
         arrived(copies_o1)
         start(copies_o2)
         cot_copy.wait_recv()
-        zf[19 * B :, :] = jnp.zeros((16 * OWN - 19 * B, L), F32)
+        zf[19 * B :, :] = jnp.zeros((32 * OWN - 19 * B, L), F32)
 
         arrived(copies_o2)
         arrived(copies_g1)
@@ -382,12 +399,15 @@
                 r0 = (c0 // L + t) * B
                 zf[r0 : r0 + B, :] = term[:, t * L : (t + 1) * L]
 
-        def flat_body(o, _):
-            F16[o // 8, o % 8] = zf[pl.ds(pl.multiple_of(o * OWN, OWN), OWN), :].astype(BF16)
-            return 0
-
-        lax.fori_loop(0, 16, flat_body, 0)
-        z1.start()
+        for e in (0, 1):
+
+            def flat_body(o, _):
+                at = pl.ds(pl.multiple_of((e * 16 + o) * OWN, OWN), OWN)
+                F16[e, o // 8, o % 8] = zf[at, :].astype(BF16)
+                return 0
+
+            lax.fori_loop(0, 16, flat_body, 0)
+            z1[e].start()
 
     @pl.when(base)
     def _():
@@ -398,16 +418,18 @@
 
     @pl.when(control)
     def _():
-        z1.wait_recv()
-
-        def pair_body(q, _):
-            total = zf[pl.ds(pl.multiple_of((c * 8 + q) * OWN, OWN), OWN), :] + zr1[q].astype(F32)
-            H32[q] = total
-            H16[q] = total.astype(BF16)
-            return 0
-
-        lax.fori_loop(0, 8, pair_body, 0)
-        start(z2)
+        for e in (0, 1):
+            z1[e].wait_recv()
+
+            def pair_body(q, _):
+                at = pl.ds(pl.multiple_of((e * 16 + c * 8 + q) * OWN, OWN), OWN)
+                total = zf[at, :] + zr1[e, q].astype(F32)
+                H32[e, q] = total
+                H16[e, q] = total.astype(BF16)
+                return 0
+
+            lax.fori_loop(0, 8, pair_body, 0)
+            start(z2[e])
 
     arrived(copies_g2)
     flatten(GG)
@@ -432,26 +454,35 @@
     st_s1[8:16, :] = p2
     start(st1)
 
-    @pl.when(control)
-    def _():
-        for k in (1, 2, 3):
-            z2_arrival((z + k) % 4).wait_recv()
-        total = H32[pos]
-        for k in (1, 2, 3):
-            total = total + zr2[(z + k) % 4].astype(F32)
-        A16[c, pos] = total.astype(BF16)
-
-    @pl.when(base)
-    def _():
-        for k in range(4):
-            z2_arrival(k).wait_recv()
-        total = zr2[0].astype(F32)
-        for k in (1, 2, 3):
-            total = total + zr2[k].astype(F32)
-        A16[c, pos] = total.astype(BF16)
-
-    start(near)
-    z4[0].start()
+    for e in (0, 1):
+
+        @pl.when(control)
+        def _():
+            for k in (1, 2, 3):
+                z2_arrival(e, (z + k) % 4).wait_recv()
+            total = H32[e, pos]
+            for k in (1, 2, 3):
+                total = total + zr2[e, (z + k) % 4].astype(F32)
+            A16[e, c, pos] = total.astype(BF16)
+
+        @pl.when(base)
+        def _():
+            for k in range(4):
+                z2_arrival(e, k).wait_recv()
+            total = zr2[e, 0].astype(F32)
+            for k in (1, 2, 3):
+                total = total + zr2[e, k].astype(F32)
+            A16[e, c, pos] = total.astype(BF16)
+
+        start(near[e])
+        z4[e][0].start()
+
+    def pass_on(e):
+        arrived(near[e])
+        start(far[e])
+        start(z4[e][1:3] + z4[e][6:8])
+
+    pass_on(0)
 
     arrived(copies_n1)
     rs_mid(sN, rN1, mN32, mN16)
@@ -459,6 +490,7 @@
     arrived(st1)
     st_s2[...] = st_s1[...] + st_r1[0] + st_r1[1] + st_r1[2]
     start(st2)
+    pass_on(1)
 
     @pl.when(base)
     def _():
@@ -467,9 +499,6 @@
         residual = jnp.dot(zw[...], a2d[...], preferred_element_type=F32)
         block_o[...] = (rows32[...] + residual).astype(BF16)
 
-    arrived(near)
-    start(far)
-    start(z4[1:3] + z4[6:8])
     arrived(copies_n2)
     arrived(st2)
     rs_last(mN32, rN2, rows32)
@@ -480,12 +509,13 @@
     ghat = rows32[...] * twice(cols[own_rows, :L])
     grad_o[...] = up32[...] + stat[1:2, :] * (ghat - m1 - xhat * m2)
 
-    arrived(far)
-    start(z4[3:6])
-    arrived(z4)
+    for e in (0, 1):
+        arrived(far[e])
+        start(z4[e][3:6])
+    arrived(z4[0] + z4[1])
 
     sent(copies_b1 + copies_b2 + copies_g1 + copies_g2 + copies_o1 + copies_o2 + copies_n1 + copies_n2)
-    sent(st1 + st2 + near + far + z4)
+    sent(st1 + st2 + near[0] + near[1] + far[0] + far[1] + z4[0] + z4[1])
 
     @pl.when(base)
     def _():
@@ -493,31 +523,28 @@
 
     @pl.when(control)
     def _():
-        sent(z2 + [co_copy, z1])
-
-
-def finish(block, grad, flat, block_o, grad_o, zero_o, flat_v, zf, rows, sem):
-    copies = [
-        pltpu.make_async_copy(flat, flat_v, sem.at[0]),
-        pltpu.make_async_copy(block, block_o.at[0], sem.at[1]),
-        pltpu.make_async_copy(grad, grad_o.at[0], sem.at[2]),
-    ]
-    for cp in copies:
+        sent(z2[0] + z2[1] + z1 + [co_copy])
+
+
+def finish(block, grad, flat, block_o, grad_o, zero_o, flat_v, zf, rows, block_v, grad_v, sem):
+    def move(src, dst, i):
+        cp = pltpu.make_async_copy(src, dst, sem.at[i])
         cp.start()
-    copies[0].wait()
-
-    def body(o, _):
-        zf[pl.ds(pl.multiple_of(o * OWN, OWN), OWN), :] = flat_v[o // 8, o % 8].astype(F32)
-        return 0
-
-    lax.fori_loop(0, 16, body, 0)
+        return cp
+
+    ins = [move(flat, flat_v, 0), move(grad, grad_v, 1), move(block, block_v, 2)]
+    ins[1].wait()
+    outs = [move(grad_v, grad_o.at[0], 3)]
+    ins[2].wait()
+    outs.append(move(block_v, block_o.at[0], 4))
+    ins[0].wait()
+    for o in range(32):
+        zf[o * OWN : (o + 1) * OWN, :] = flat_v[o // 16, (o // 8) % 2, o % 8].astype(F32)
     for t in range(19):
         rows[:, t * L : (t + 1) * L] = zf[t * B : (t + 1) * B, :]
-    out = pltpu.make_async_copy(rows, zero_o, sem.at[3])
-    out.start()
-    out.wait()
-    copies[1].wait()
-    copies[2].wait()
+    outs.append(move(rows, zero_o, 5))
+    for cp in outs:
+        cp.wait()
 
 
 def local(acts, modulation, w_in, w_out, zero_weight, cotangent):
@@ -534,17 +561,17 @@
         vm((2, 4, 4, B, L), BF16), vm((2, 4, 4, B, L), BF16), vm((D, N), BF16), vm((B, N), F32), vm((B, N), F32),
         vm((B, N), BF16), vm((B, N), BF16), vm((B, N), BF16), vm((B, N), BF16),
         vm((16, N), F32), vm((3, 16, N), F32), vm((16, N), F32), vm((3, 16, N), F32),
-        vm((B, N), BF16), vm((16 * OWN, L), F32), vm((2, 8, OWN, L), BF16), vm((8, OWN, L), BF16), vm((8, OWN, L), F32), vm((8, OWN, L), BF16),
-        vm((4, OWN, L), BF16),
-        dma((10, 2, 3)), dma((10, 2, 3)), dma((2, 3)), dma((2, 3)), dma((3,)), dma((3,)), dma((9,)), dma((9,)),
-        dma((7,)), dma((4,)), dma((8,)), dma((8,)),
+        vm((B, N), BF16), vm((32 * OWN, L), F32), vm((2, 2, 8, OWN, L), BF16), vm((2, 8, OWN, L), BF16), vm((2, 8, OWN, L), F32),
+        vm((2, 8, OWN, L), BF16), vm((2, 4, OWN, L), BF16),
+        dma((10, 2, 3)), dma((10, 2, 3)), dma((2, 3)), dma((2, 3)), dma((3,)), dma((3,)), dma((2,)), dma((2,)),
+        dma((2, 7)), dma((2, 4)), dma((2, 8)), dma((2, 8)), dma((2, 8)), dma((2, 8)),
     ]
     results = pl.pallas_call(
         kernel,
         out_shape=(
             jax.ShapeDtypeStruct((B, N), BF16),
             jax.ShapeDtypeStruct((B, N), F32),
-            jax.ShapeDtypeStruct((2, 8, OWN, L), BF16),
+            jax.ShapeDtypeStruct((2, 2, 8, OWN, L), BF16),
         ),
         in_specs=[pl.BlockSpec(memory_space=pl.ANY)] * 6,
         out_specs=[pl.BlockSpec(memory_space=pltpu.VMEM)] * 3,
@@ -562,7 +589,7 @@
         ),
         in_specs=[pl.BlockSpec(memory_space=pl.ANY)] * 3,
         out_specs=[pl.BlockSpec(memory_space=pl.ANY)] * 3,
-        scratch_shapes=[vm((2, 8, OWN, L), BF16), vm((16 * OWN, L), F32), vm((B, D), F32), dma((4,))],
+        scratch_shapes=[vm((2, 2, 8, OWN, L), BF16), vm((32 * OWN, L), F32), vm((B, D), F32), vm((B, N), BF16), vm((B, N), F32), dma((6,))],
         compiler_params=pltpu.CompilerParams(vmem_limit_bytes=60 * 2**20),
     )(*results)
 

time: 78 us -> 69.9 us (0.90)
  Pallas kernels: 77.2 us -> 69.1 us
    pallas_call x1, Pallas kernels: 8.21 us -> 2.43 us  [local(): pl.pallas_call(finish, out_shape=(jax.ShapeDtypeStruct((1, B, N), BF16),...]
    pallas_call x1, Pallas kernels: 69 us -> 66.7 us  [local(): pl.pallas_call(kernel, out_shape=(jax.ShapeDtypeStruct((B, N), BF16), jax...]
where the time goes in v4:
time: 69.9 us; the launch traced here: 69.8 us
  Pallas kernels  69.1 us (99%)
    pallas_call x1, Pallas kernels, local(): pl.pallas_call(kernel, out_shape=(jax.ShapeDtypeStruct((B, N), BF16), jax...  66.7 us
    pallas_call x1, Pallas kernels, local(): pl.pallas_call(finish, out_shape=(jax.ShapeDtypeStruct((1, B, N), BF16),...  2.43 us

profile of v4, /device:TPU:1, one launch (start us, length us, event | category | flops | bytes accessed | tf_op | source)
XLA Modules:
  0.0 69.8 jit_solution(16904134387443300216)
XLA Ops:
  0.6 66.7 %shard_map.85 = (bf16[152,256]{1,0:T(8,128)(2,1)}, f32[152,256]{1,0:T(8,128)}, bf16[2,2,8,96,128]{4,3,2,1,0:T(8,128)(2,1)}) custom-call(bf16[1,2432,256]{2,1,0:T(8,128)(2,1)} %acts_h.1, f32[3,1,2432]{2,1,0:T(1,128)} %bitcast.1, bf16[1,608,2432]{2,1,0:T(8,128)(2,1)} %win_h.1, bf16[1,608,2432]{2,1,0:T(8,128)(2,1)} %wout_h.1, bf16[152,2432]{1,0:T(8,128)(2,1)} %zw_h.1, ...), custom_call_target="tpu_custom_call" | custom-call | tf_op jit(solution)/shard_map/pallas_call | solution.py:569
  67.3 2.4 %shard_map.86 = (bf16[1,152,256]{2,1,0:T(8,128)(2,1)}, f32[1,152,256]{2,1,0:T(8,128)}, f32[152,2432]{1,0:T(8,128)}) custom-call(bf16[152,256]{1,0:T(8,128)(2,1)} %get-tuple-element.6.block, f32[152,256]{1,0:T(8,128)} %get-tuple-element.7.grad, bf16[2,2,8,96,128]{4,3,2,1,0:T(8,128)(2,1)} %get-tuple-element.8.flat), custom_call_target="tpu_custom_call" | custom-call | tf_op jit(solution)/shard_map/pallas_call | solution.py:583

commit v5 on v4

--- a/solution.py
+++ b/solution.py
@@ -16,7 +16,8 @@
 H = 608
 N = 256
 L = 128
-OWN = 96
+E = 2
+OWN = 192 // E
 GELU_C = 0.7978845608028654
 TILES = ((0, 640), (640, 640), (1280, 640), (1920, 512))
 
@@ -129,6 +130,21 @@
             out.append(remote(blk, blk, ss.at[n, h, k - 1], rs.at[n, h, k - 1], where))
         return out
 
+    def ag_block(n, G, h, j):
+        if h == 0:
+            blk = G.at[0, x, (y + 4 - j) % 4]
+            return [remote(blk, blk, ss.at[n, 0, k - 1], rs.at[n, 0, k - 1], peer_x(k)) for k in (1, 3, 2)]
+        blk = G.at[1, y, (x + 4 - j) % 4]
+        return [remote(blk, blk, ss.at[n, 1, k - 1], rs.at[n, 1, k - 1], peer_y(k)) for k in (1, 3, 2)]
+
+    def ag_start(n, G):
+        start(ag1(n, G) + ag_block(n + 1, G, 0, 0) + ag_block(n + 1, G, 1, 0))
+
+    def ag_forward(n, G):
+        for (h, j), cp in zip(HK, ag1(n, G)):
+            cp.wait_recv()
+            start(ag_block(n + 1, G, h, j))
+
     def start(copies):
         for cp in copies:
             cp.start()
@@ -192,7 +208,7 @@
     cot_copy = remote(cot, cot1_r, g_ss.at[2], g_rs.at[2], partner)
     st1 = [remote(st_s1, st_r1.at[k - 1], st_ss.at[0, k - 1], st_rs.at[0, k - 1], peer_x(k)) for k in (1, 2, 3)]
     st2 = [remote(st_s2, st_r2.at[k - 1], st_ss.at[1, k - 1], st_rs.at[1, k - 1], peer_y(k)) for k in (1, 2, 3)]
-    z1 = [remote(F16.at[e, 1 - c], zr1.at[e], c_ss.at[e], c_rs.at[e], sibling) for e in (0, 1)]
+    z1 = [remote(F16.at[e, 1 - c], zr1.at[e], c_ss.at[e], c_rs.at[e], sibling) for e in range(E)]
     z2 = [
         [
             remote(
@@ -200,24 +216,13 @@
             )
             for k in (1, 7, 2, 6, 3, 5, 4)
         ]
-        for e in (0, 1)
+        for e in range(E)
     ]
 
     def z3_copy(e, i, blk, q):
         return remote(blk, blk, z3_ss.at[e, i], z3_rs.at[e, i], at_z(q % 8))
 
-    below, above = (pos + 6) % 8, (pos + 2) % 8
-    hw = OWN // 2
-    near = [[z3_copy(e, i, A16.at[e, c, pos], pos + by) for i, by in enumerate((1, 7, 2, 6))] for e in (0, 1)]
-    far = [
-        [
-            z3_copy(e, 4, A16.at[e, c, below], pos + 1),
-            z3_copy(e, 5, A16.at[e, c, above], pos + 7),
-            z3_copy(e, 6, A16.at[e, c, below, pl.ds(0, hw)], pos + 2),
-            z3_copy(e, 7, A16.at[e, c, above, pl.ds(hw, hw)], pos + 6),
-        ]
-        for e in (0, 1)
-    ]
+    near = [[z3_copy(e, i, A16.at[e, c, pos], pos + by) for i, by in enumerate((1, 7, 2, 6, 3, 5, 4))] for e in range(E)]
     z4 = [
         [
             remote(
@@ -225,7 +230,7 @@
             )
             for k in range(8)
         ]
-        for e in (0, 1)
+        for e in range(E)
     ]
 
     def z2_arrival(e, zz):
@@ -240,10 +245,9 @@
             T[c0 : c0 + width, :] = contract_rows(zw[:, c0 : c0 + width], cot[...])
         extract(sC)
 
-    pl.semaphore_wait(barrier, 14)
-
-    @pl.when(base)
-    def _():
+    @pl.when(base)
+    def _():
+        pl.semaphore_wait(barrier, 14)
         start(copies_c1)
         cot_copy.start()
 
@@ -334,6 +338,10 @@
                     s.at[1, yy], r1.at[1, k - 1], ss.at[n, 1, k - 1], rs.at[n, 1, k - 1], at_xy(yy, x)
                 ).start()
 
+    @pl.when(control)
+    def _():
+        pl.semaphore_wait(barrier, 14)
+
     produce(B1, wout, sB, rB1, control)
 
     own_rows = pl.ds(pl.multiple_of(f * B, 8), B)
@@ -376,16 +384,15 @@
         co_copy.start()
         GO[0, x, y] = out[:, :L]
         GO[1, y, x] = out[:, L:]
-        start(copies_o1)
+        ag_start(O1, GO)
         carr_copy.wait_recv()
         up = carr_r[...].astype(F32) + cot[...].astype(F32)
         up32[...] = up
         set_gate_grad(up)
         start(copies_g1)
-        arrived(copies_o1)
-        start(copies_o2)
+        ag_forward(O1, GO)
         cot_copy.wait_recv()
-        zf[19 * B :, :] = jnp.zeros((32 * OWN - 19 * B, L), F32)
+        zf[19 * B :, :] = jnp.zeros((16 * E * OWN - 19 * B, L), F32)
 
         arrived(copies_o2)
         arrived(copies_g1)
@@ -399,7 +406,7 @@
                 r0 = (c0 // L + t) * B
                 zf[r0 : r0 + B, :] = term[:, t * L : (t + 1) * L]
 
-        for e in (0, 1):
+        for e in range(E):
 
             def flat_body(o, _):
                 at = pl.ds(pl.multiple_of((e * 16 + o) * OWN, OWN), OWN)
@@ -418,7 +425,7 @@
 
     @pl.when(control)
     def _():
-        for e in (0, 1):
+        for e in range(E):
             z1[e].wait_recv()
 
             def pair_body(q, _):
@@ -454,7 +461,7 @@
     st_s1[8:16, :] = p2
     start(st1)
 
-    for e in (0, 1):
+    for e in range(E):
 
         @pl.when(control)
         def _():
@@ -477,20 +484,12 @@
         start(near[e])
         z4[e][0].start()
 
-    def pass_on(e):
-        arrived(near[e])
-        start(far[e])
-        start(z4[e][1:3] + z4[e][6:8])
-
-    pass_on(0)
-
     arrived(copies_n1)
     rs_mid(sN, rN1, mN32, mN16)
     start(copies_n2)
     arrived(st1)
     st_s2[...] = st_s1[...] + st_r1[0] + st_r1[1] + st_r1[2]
     start(st2)
-    pass_on(1)
 
     @pl.when(base)
     def _():
@@ -498,6 +497,10 @@
         flatten(GO)
         residual = jnp.dot(zw[...], a2d[...], preferred_element_type=F32)
         block_o[...] = (rows32[...] + residual).astype(BF16)
+
+    for e in range(E):
+        arrived(near[e])
+        start(z4[e][1:])
 
     arrived(copies_n2)
     arrived(st2)
@@ -509,13 +512,13 @@
     ghat = rows32[...] * twice(cols[own_rows, :L])
     grad_o[...] = up32[...] + stat[1:2, :] * (ghat - m1 - xhat * m2)
 
-    for e in (0, 1):
-        arrived(far[e])
-        start(z4[e][3:6])
-    arrived(z4[0] + z4[1])
+    for e in range(E):
+        arrived(z4[e])
 
     sent(copies_b1 + copies_b2 + copies_g1 + copies_g2 + copies_o1 + copies_o2 + copies_n1 + copies_n2)
-    sent(st1 + st2 + near[0] + near[1] + far[0] + far[1] + z4[0] + z4[1])
+    sent(st1 + st2)
+    for e in range(E):
+        sent(near[e] + z4[e])
 
     @pl.when(base)
     def _():
@@ -523,7 +526,9 @@
 
     @pl.when(control)
     def _():
-        sent(z2[0] + z2[1] + z1 + [co_copy])
+        sent(z1 + [co_copy])
+        for e in range(E):
+            sent(z2[e])
 
 
 def finish(block, grad, flat, block_o, grad_o, zero_o, flat_v, zf, rows, block_v, grad_v, sem):
@@ -538,7 +543,7 @@
     ins[2].wait()
     outs.append(move(block_v, block_o.at[0], 4))
     ins[0].wait()
-    for o in range(32):
+    for o in range(16 * E):
         zf[o * OWN : (o + 1) * OWN, :] = flat_v[o // 16, (o // 8) % 2, o % 8].astype(F32)
     for t in range(19):
         rows[:, t * L : (t + 1) * L] = zf[t * B : (t + 1) * B, :]
@@ -561,17 +566,17 @@
         vm((2, 4, 4, B, L), BF16), vm((2, 4, 4, B, L), BF16), vm((D, N), BF16), vm((B, N), F32), vm((B, N), F32),
         vm((B, N), BF16), vm((B, N), BF16), vm((B, N), BF16), vm((B, N), BF16),
         vm((16, N), F32), vm((3, 16, N), F32), vm((16, N), F32), vm((3, 16, N), F32),
-        vm((B, N), BF16), vm((32 * OWN, L), F32), vm((2, 2, 8, OWN, L), BF16), vm((2, 8, OWN, L), BF16), vm((2, 8, OWN, L), F32),
-        vm((2, 8, OWN, L), BF16), vm((2, 4, OWN, L), BF16),
-        dma((10, 2, 3)), dma((10, 2, 3)), dma((2, 3)), dma((2, 3)), dma((3,)), dma((3,)), dma((2,)), dma((2,)),
-        dma((2, 7)), dma((2, 4)), dma((2, 8)), dma((2, 8)), dma((2, 8)), dma((2, 8)),
+        vm((B, N), BF16), vm((16 * E * OWN, L), F32), vm((E, 2, 8, OWN, L), BF16), vm((E, 8, OWN, L), BF16),
+        vm((E, 8, OWN, L), F32), vm((E, 8, OWN, L), BF16), vm((E, 4, OWN, L), BF16),
+        dma((10, 2, 3)), dma((10, 2, 3)), dma((2, 3)), dma((2, 3)), dma((3,)), dma((3,)), dma((E,)), dma((E,)),
+        dma((E, 7)), dma((E, 4)), dma((E, 7)), dma((E, 7)), dma((E, 8)), dma((E, 8)),
     ]
     results = pl.pallas_call(
         kernel,
         out_shape=(
             jax.ShapeDtypeStruct((B, N), BF16),
             jax.ShapeDtypeStruct((B, N), F32),
-            jax.ShapeDtypeStruct((2, 2, 8, OWN, L), BF16),
+            jax.ShapeDtypeStruct((E, 2, 8, OWN, L), BF16),
         ),
         in_specs=[pl.BlockSpec(memory_space=pl.ANY)] * 6,
         out_specs=[pl.BlockSpec(memory_space=pltpu.VMEM)] * 3,
@@ -589,7 +594,7 @@
         ),
         in_specs=[pl.BlockSpec(memory_space=pl.ANY)] * 3,
         out_specs=[pl.BlockSpec(memory_space=pl.ANY)] * 3,
-        scratch_shapes=[vm((2, 2, 8, OWN, L), BF16), vm((32 * OWN, L), F32), vm((B, D), F32), vm((B, N), BF16), vm((B, N), F32), dma((6,))],
+        scratch_shapes=[vm((E, 2, 8, OWN, L), BF16), vm((16 * E * OWN, L), F32), vm((B, D), F32), vm((B, N), BF16), vm((B, N), F32), dma((6,))],
         compiler_params=pltpu.CompilerParams(vmem_limit_bytes=60 * 2**20),
     )(*results)
 

time: 69.9 us -> 67 us (0.959)
  Pallas kernels: 69.1 us -> 66.2 us
    pallas_call x1, Pallas kernels: 66.7 us -> 63.8 us  [local(): pl.pallas_call(kernel, out_shape=(jax.ShapeDtypeStruct((B, N), BF16), jax...]
where the time goes in v5:
time: 67 us; the launch traced here: 66.9 us
  Pallas kernels  66.2 us (99%)
    pallas_call x1, Pallas kernels, local(): pl.pallas_call(kernel, out_shape=(jax.ShapeDtypeStruct((B, N), BF16), jax...  63.8 us
    pallas_call x1, Pallas kernels, local(): pl.pallas_call(finish, out_shape=(jax.ShapeDtypeStruct((1, B, N), BF16),...  2.43 us

profile of v5, /device:TPU:1, one launch (start us, length us, event | category | flops | bytes accessed | tf_op | source)
XLA Modules:
  0.0 66.9 jit_solution(6643464145165635325)
XLA Ops:
  0.6 63.8 %shard_map.85 = (bf16[152,256]{1,0:T(8,128)(2,1)}, f32[152,256]{1,0:T(8,128)}, bf16[2,2,8,96,128]{4,3,2,1,0:T(8,128)(2,1)}) custom-call(bf16[1,2432,256]{2,1,0:T(8,128)(2,1)} %acts_h.1, f32[3,1,2432]{2,1,0:T(1,128)} %bitcast.1, bf16[1,608,2432]{2,1,0:T(8,128)(2,1)} %win_h.1, bf16[1,608,2432]{2,1,0:T(8,128)(2,1)} %wout_h.1, bf16[152,2432]{1,0:T(8,128)(2,1)} %zw_h.1, ...), custom_call_target="tpu_custom_call" | custom-call | tf_op jit(solution)/shard_map/pallas_call | solution.py:574
  64.4 2.4 %shard_map.86 = (bf16[1,152,256]{2,1,0:T(8,128)(2,1)}, f32[1,152,256]{2,1,0:T(8,128)}, f32[152,2432]{1,0:T(8,128)}) custom-call(bf16[152,256]{1,0:T(8,128)(2,1)} %get-tuple-element.6.block, f32[152,256]{1,0:T(8,128)} %get-tuple-element.7.grad, bf16[2,2,8,96,128]{4,3,2,1,0:T(8,128)(2,1)} %get-tuple-element.8.flat), custom_call_target="tpu_custom_call" | custom-call | tf_op jit(solution)/shard_map/pallas_call | solution.py:588

commit v6 on v5

--- a/solution.py
+++ b/solution.py
@@ -369,15 +369,20 @@
         arrived(copies_g1)
         start(copies_g2)
 
-    arrived(copies_b1)
-    rs_mid(sB, rB1, mB32, mB16)
-    start(copies_b2)
-    arrived(copies_b2)
-    rs_last(mB32, rB2, rows32)
-    rows32[...] = xf[own_rows, :] + gate_rows * rows32[...]
+    def branch_mid():
+        arrived(copies_b1)
+        rs_mid(sB, rB1, mB32, mB16)
+        start(copies_b2)
+
+    def branch_rows():
+        arrived(copies_b2)
+        rs_last(mB32, rB2, rows32)
+        rows32[...] = xf[own_rows, :] + gate_rows * rows32[...]
 
     @pl.when(control)
     def _():
+        branch_mid()
+        branch_rows()
         out = rows32[...].astype(BF16)
         block_o[...] = out
         co_s[...] = out
@@ -461,6 +466,10 @@
     st_s1[8:16, :] = p2
     start(st1)
 
+    @pl.when(base)
+    def _():
+        branch_mid()
+
     for e in range(E):
 
         @pl.when(control)
@@ -493,14 +502,16 @@
 
     @pl.when(base)
     def _():
+        branch_rows()
         arrived(copies_o2)
         flatten(GO)
         residual = jnp.dot(zw[...], a2d[...], preferred_element_type=F32)
         block_o[...] = (rows32[...] + residual).astype(BF16)
 
     for e in range(E):
-        arrived(near[e])
-        start(z4[e][1:])
+        for cp, k in zip(near[e], (7, 1, 6, 2, 5, 3, 4)):
+            cp.wait_recv()
+            z4[e][k].start()
 
     arrived(copies_n2)
     arrived(st2)

time: 67 us -> 66.6 us (level)
  no operation moved by 1% of the time
where the time goes in v6:
time: 66.6 us; the launch traced here: 66.5 us
  Pallas kernels  65.8 us (99%)
    pallas_call x1, Pallas kernels, local(): pl.pallas_call(kernel, out_shape=(jax.ShapeDtypeStruct((B, N), BF16), jax...  63.4 us
    pallas_call x1, Pallas kernels, local(): pl.pallas_call(finish, out_shape=(jax.ShapeDtypeStruct((1, B, N), BF16),...  2.43 us

profile of v6, /device:TPU:1, one launch (start us, length us, event | category | flops | bytes accessed | tf_op | source)
XLA Modules:
  0.0 66.5 jit_solution(15189082573082830936)
XLA Ops:
  0.6 63.4 %shard_map.85 = (bf16[152,256]{1,0:T(8,128)(2,1)}, f32[152,256]{1,0:T(8,128)}, bf16[2,2,8,96,128]{4,3,2,1,0:T(8,128)(2,1)}) custom-call(bf16[1,2432,256]{2,1,0:T(8,128)(2,1)} %acts_h.1, f32[3,1,2432]{2,1,0:T(1,128)} %bitcast.1, bf16[1,608,2432]{2,1,0:T(8,128)(2,1)} %win_h.1, bf16[1,608,2432]{2,1,0:T(8,128)(2,1)} %wout_h.1, bf16[152,2432]{1,0:T(8,128)(2,1)} %zw_h.1, ...), custom_call_target="tpu_custom_call" | custom-call | tf_op jit(solution)/shard_map/pallas_call | solution.py:585
  64.0 2.4 %shard_map.86 = (bf16[1,152,256]{2,1,0:T(8,128)(2,1)}, f32[1,152,256]{2,1,0:T(8,128)}, f32[152,2432]{1,0:T(8,128)}) custom-call(bf16[152,256]{1,0:T(8,128)(2,1)} %get-tuple-element.6.block, f32[152,256]{1,0:T(8,128)} %get-tuple-element.7.grad, bf16[2,2,8,96,128]{4,3,2,1,0:T(8,128)(2,1)} %get-tuple-element.8.flat), custom_call_target="tpu_custom_call" | custom-call | tf_op jit(solution)/shard_map/pallas_call | solution.py:599

commit v7 on v6

--- a/solution.py
+++ b/solution.py
@@ -554,11 +554,13 @@
     ins[2].wait()
     outs.append(move(block_v, block_o.at[0], 4))
     ins[0].wait()
-    for o in range(16 * E):
-        zf[o * OWN : (o + 1) * OWN, :] = flat_v[o // 16, (o // 8) % 2, o % 8].astype(F32)
-    for t in range(19):
-        rows[:, t * L : (t + 1) * L] = zf[t * B : (t + 1) * B, :]
-    outs.append(move(rows, zero_o, 5))
+    for i, (o0, o1, t0, t1) in enumerate(((0, 16, 0, 10), (16, 32, 10, 19))):
+        for o in range(o0, o1):
+            zf[o * OWN : (o + 1) * OWN, :] = flat_v[o // 16, (o // 8) % 2, o % 8].astype(F32)
+        for t in range(t0, t1):
+            rows[:, t * L : (t + 1) * L] = zf[t * B : (t + 1) * B, :]
+        part = pl.ds(t0 * L, (t1 - t0) * L)
+        outs.append(move(rows.at[:, part], zero_o.at[:, part], 5 + i))
     for cp in outs:
         cp.wait()
 
@@ -605,7 +607,7 @@
         ),
         in_specs=[pl.BlockSpec(memory_space=pl.ANY)] * 3,
         out_specs=[pl.BlockSpec(memory_space=pl.ANY)] * 3,
-        scratch_shapes=[vm((E, 2, 8, OWN, L), BF16), vm((16 * E * OWN, L), F32), vm((B, D), F32), vm((B, N), BF16), vm((B, N), F32), dma((6,))],
+        scratch_shapes=[vm((E, 2, 8, OWN, L), BF16), vm((16 * E * OWN, L), F32), vm((B, D), F32), vm((B, N), BF16), vm((B, N), F32), dma((7,))],
         compiler_params=pltpu.CompilerParams(vmem_limit_bytes=60 * 2**20),
     )(*results)
 

time: 66.6 us -> 66.5 us (level)
  no operation moved by 1% of the time
where the time goes in v7:
time: 66.5 us; the launch traced here: 66.4 us
  Pallas kernels  65.8 us (99%)
    pallas_call x1, Pallas kernels, local(): pl.pallas_call(kernel, out_shape=(jax.ShapeDtypeStruct((B, N), BF16), jax...  63.4 us
    pallas_call x1, Pallas kernels, local(): pl.pallas_call(finish, out_shape=(jax.ShapeDtypeStruct((1, B, N), BF16),...  2.39 us

profile of v7, /device:TPU:1, one launch (start us, length us, event | category | flops | bytes accessed | tf_op | source)
XLA Modules:
  0.0 66.4 jit_solution(6247215611294173830)
XLA Ops:
  0.6 63.4 %shard_map.85 = (bf16[152,256]{1,0:T(8,128)(2,1)}, f32[152,256]{1,0:T(8,128)}, bf16[2,2,8,96,128]{4,3,2,1,0:T(8,128)(2,1)}) custom-call(bf16[1,2432,256]{2,1,0:T(8,128)(2,1)} %acts_h.1, f32[3,1,2432]{2,1,0:T(1,128)} %bitcast.1, bf16[1,608,2432]{2,1,0:T(8,128)(2,1)} %win_h.1, bf16[1,608,2432]{2,1,0:T(8,128)(2,1)} %wout_h.1, bf16[152,2432]{1,0:T(8,128)(2,1)} %zw_h.1, ...), custom_call_target="tpu_custom_call" | custom-call | tf_op jit(solution)/shard_map/pallas_call | solution.py:587
  64.0 2.4 %shard_map.86 = (bf16[1,152,256]{2,1,0:T(8,128)(2,1)}, f32[1,152,256]{2,1,0:T(8,128)}, f32[152,2432]{1,0:T(8,128)}) custom-call(bf16[152,256]{1,0:T(8,128)(2,1)} %get-tuple-element.6.block, f32[152,256]{1,0:T(8,128)} %get-tuple-element.7.grad, bf16[2,2,8,96,128]{4,3,2,1,0:T(8,128)(2,1)} %get-tuple-element.8.flat), custom_call_target="tpu_custom_call" | custom-call | tf_op jit(solution)/shard_map/pallas_call | solution.py:601
